TPU v7x, 128 devices: a whole 4x4x4 slice. The times are simulated.
128 devices in a mesh: seq: 32 (over z, x, core), head: 4 (over y).
Axes of the slice: x: 4, y: 4, z: 4, core: 2. Of those that a mesh axis runs over, the one named last changes fastest.
Arguments:
- query_in: bfloat16 [32768, 2048], P(('seq', 'head')), may hold values from -12 to 12
- key_in: bfloat16 [32768, 2048], P(('seq', 'head')), may hold values from -12 to 12
- value_in: bfloat16 [32768, 2048], P(('seq', 'head')), may hold values from -6 to 6
- out_grad: bfloat16 [32768, 2048], P(('seq', 'head')), may hold values from -6 to 6
- pattern: int32 [256, 256], replicated, may hold values from 0 to 1, as said below
Outputs:
- attended: bfloat16 [32768, 2048], P(('seq', 'head'))
- query_grad: bfloat16 [32768, 2048], P(('seq', 'head'))
- key_grad: bfloat16 [32768, 2048], P(('seq', 'head'))
- value_grad: bfloat16 [32768, 2048], P(('seq', 'head'))
Inputs may be any that keep to these rules, and one draw needn't show every extreme that they name: `pattern`: Symmetric. Row 0, column 0 and every entry with |a - b| <= 1 are 1. Every other 1 at (a, b) joins blocks of two different groups of 8 consecutive blocks, and two groups share at most one such pair.
All inputs are finite; a program needn't handle non-finite values.
Results may differ from a plain program's by a relative error of at most 0.0075.
The roundings to bfloat16 on the way count: a program that leaves them out, or rounds other values in their place, can miss the bound.
Values may be sent and summed in bfloat16 or wider, within the bound.
A program may use at most 256 MiB of HBM per device.

v0:
```python
import jax
import jax.numpy as jnp
from jax import lax
from jax.sharding import PartitionSpec as P

HEAD_DIM = 128
BLOCK = 128


big_negative = -1e30
highest = lax.Precision.HIGHEST


def spread(block, axis, holder):
    block = jnp.where(lax.axis_index(axis) == holder, block, jnp.zeros_like(block))
    return lax.psum(block, axis)


def with_halo(block, sides, width):
    for axis, dim in sides:
        count = lax.axis_size(axis)
        forward = [(i, i + 1) for i in range(count - 1)]
        backward = [(target, source) for source, target in forward]
        low = lax.ppermute(
            lax.slice_in_dim(block, block.shape[dim] - width, None, axis=dim), axis, forward
        )
        high = lax.ppermute(lax.slice_in_dim(block, 0, width, axis=dim), axis, backward)
        block = jnp.concatenate([low, block, high], axis=dim)
    return block


def passed_along(block, axis, distance):
    devices = range(lax.axis_size(axis))
    route = [(i - distance, i) for i in devices if i - distance in devices]
    return lax.ppermute(block, axis, route)


def link_tables(own_rows, own_index, shards, per_dev):
    linked_rows = own_rows.reshape(per_dev, shards, per_dev)
    own_block = jnp.arange(per_dev, dtype=jnp.int32)[:, None, None]
    peer_index = jnp.arange(shards, dtype=jnp.int32)[None, :, None]
    peer_block = jnp.arange(per_dev, dtype=jnp.int32)[None, None, :]
    own_id = own_index * per_dev + own_block
    peer_id = peer_index * per_dev + peer_block
    linked = (peer_index != own_index) & (linked_rows > 0) & (own_id > 0) & (peer_id > 0)
    far_link = jnp.abs(own_id - peer_id) > 1
    take_mask = linked & far_link
    give_mask = linked & far_link
    recv_live = jnp.sum(take_mask.astype(jnp.int32), axis=(0, 2))
    recv_block = jnp.sum(take_mask.astype(jnp.int32) * own_block, axis=(0, 2))
    send_live = jnp.sum(give_mask.astype(jnp.int32), axis=(0, 2))
    send_block = jnp.sum(give_mask.astype(jnp.int32) * own_block, axis=(0, 2))
    return (recv_live, recv_block, send_live, send_block)


def band_stack(padded_blocks, global_rows, per_dev):
    global_tile = jnp.broadcast_to(global_rows[None], (per_dev,) + global_rows.shape)
    tiles = jnp.stack(
        (
            padded_blocks[0:per_dev],
            padded_blocks[1 : per_dev + 1],
            padded_blocks[2 : per_dev + 2],
            global_tile,
        ),
        axis=1,
    )
    return tiles.reshape((per_dev, 4 * global_rows.shape[0]) + global_rows.shape[1:])


def band_return(band_terms, per_dev, block_rows):
    split_terms = band_terms.reshape((per_dev, 4, block_rows) + band_terms.shape[2:])
    tail = ((0, 0),) * (split_terms.ndim - 2)
    padded_terms = jnp.pad(split_terms[:, 0], ((0, 2),) + tail)
    padded_terms = padded_terms + jnp.pad(split_terms[:, 1], ((1, 1),) + tail)
    padded_terms = padded_terms + jnp.pad(split_terms[:, 2], ((2, 0),) + tail)
    global_terms = jnp.sum(split_terms[:, 3], axis=0)
    flat_shape = (-1,) + band_terms.shape[2:]
    return jnp.concatenate((padded_terms.reshape(flat_shape), global_terms), axis=0)


def body(query_in, key_in, value_in, out_grad, pattern):
    query_all, key_all, value_all, grad_all = (
        lax.all_to_all(query_in, "head", split_axis=1, concat_axis=0, tiled=True),
        lax.all_to_all(key_in, "head", split_axis=1, concat_axis=0, tiled=True),
        lax.all_to_all(value_in, "head", split_axis=1, concat_axis=0, tiled=True),
        lax.all_to_all(out_grad, "head", split_axis=1, concat_axis=0, tiled=True),
    )
    frames, width_dev = query_all.shape
    block_rows = BLOCK
    head_count = width_dev // HEAD_DIM
    per_dev = frames // block_rows
    shards = lax.axis_size("seq")
    own_index = lax.axis_index("seq")
    total_blocks = shards * per_dev
    score_scale = HEAD_DIM ** (-0.5)
    head_shape = (frames, head_count, HEAD_DIM)
    block_shape = (per_dev, block_rows, head_count, HEAD_DIM)
    tile_shape = (block_rows, head_count, HEAD_DIM)
    key_heads = key_all.reshape(head_shape)
    value_heads = value_all.reshape(head_shape)
    grad_heads = grad_all.reshape(head_shape)
    query_blocks = query_all.reshape(block_shape)
    key_blocks = key_all.reshape(block_shape)
    value_blocks = value_all.reshape(block_shape)
    grad_blocks = grad_all.reshape(block_shape)
    own_rows = lax.dynamic_slice_in_dim(pattern, own_index * per_dev, per_dev, 0)
    recv_live, recv_block, send_live, send_block = link_tables(own_rows, own_index, shards, per_dev)
    block_ids = jnp.arange(per_dev, dtype=jnp.int32)
    slot_rows = ((recv_block[:, None] == block_ids[None, :]) & (recv_live[:, None] > 0)).astype(
        jnp.float32
    )
    give_rows = ((send_block[:, None] == block_ids[None, :]) & (send_live[:, None] > 0)).astype(
        jnp.float32
    )
    global_query, global_key, global_value, global_grad = (
        spread(query_all[:block_rows], "seq", 0),
        spread(key_all[:block_rows], "seq", 0),
        spread(value_all[:block_rows], "seq", 0),
        spread(grad_all[:block_rows], "seq", 0),
    )
    padded = with_halo(jnp.stack((key_all, value_all)), (("seq", 1),), block_rows)
    padded_key_blocks = padded[0].reshape((per_dev + 2,) + tile_shape)
    padded_value_blocks = padded[1].reshape((per_dev + 2,) + tile_shape)
    band_keys = band_stack(padded_key_blocks, global_key.reshape(tile_shape), per_dev)
    band_values = band_stack(padded_value_blocks, global_value.reshape(tile_shape), per_dev)
    slot_key, slot_value = (
        lax.all_to_all(
            jnp.take(key_blocks, send_block, axis=0), "seq", split_axis=0, concat_axis=0, tiled=True
        ),
        lax.all_to_all(
            jnp.take(value_blocks, send_block, axis=0),
            "seq",
            split_axis=0,
            concat_axis=0,
            tiled=True,
        ),
    )
    offsets = own_index * per_dev - 1 + jnp.arange(per_dev + 2, dtype=jnp.int32)
    col_block = jnp.concatenate((offsets, jnp.zeros((1,), jnp.int32)))
    col_live = jnp.concatenate(
        ((offsets > 0) & (offsets < total_blocks), jnp.ones((1,), jnp.bool_))
    )
    near_mask = (
        jnp.take(own_rows, jnp.clip(col_block, 0, total_blocks - 1), axis=1) > 0
    ) & col_live[None, :]
    band_index = jnp.concatenate(
        (
            block_ids[:, None] + jnp.arange(3, dtype=jnp.int32)[None, :],
            jnp.full((per_dev, 1), per_dev + 2, jnp.int32),
        ),
        axis=1,
    )
    band_mask = jnp.take_along_axis(near_mask, band_index, axis=1)
    band_live = jnp.broadcast_to(band_mask[:, :, None], (per_dev, 4, block_rows)).reshape(
        per_dev, 4 * block_rows
    )
    row_live = own_index * per_dev + block_ids > 0
    slot_mask = recv_live > 0
    near_scores = (
        jnp.einsum("nqhe,nkhe->hnqk", query_blocks, band_keys, preferred_element_type=jnp.float32)
        * score_scale
    )
    near_scores = jnp.where(band_live[None, :, None, :], near_scores, big_negative)
    slot_query = jnp.take(query_blocks, recv_block, axis=0)
    slot_scores = (
        jnp.einsum("nqhe,nkhe->hnqk", slot_query, slot_key, preferred_element_type=jnp.float32)
        * score_scale
    )
    slot_scores = jnp.where(slot_mask[None, :, None, None], slot_scores, big_negative)
    near_top = jnp.max(near_scores, axis=3)
    slot_top = jnp.max(slot_scores, axis=3)
    slot_top_rows = jnp.max(
        jnp.where(slot_rows[None, :, :, None] > 0, slot_top[:, :, None, :], big_negative), axis=1
    )
    row_top = jnp.maximum(near_top, slot_top_rows)
    near_total = jnp.sum(jnp.exp(near_scores - row_top[:, :, :, None]), axis=3)
    slot_exp = jnp.exp(slot_scores - jnp.take(row_top, recv_block, axis=1)[:, :, :, None])
    slot_total = jnp.einsum("hnq,ni->hiq", jnp.sum(slot_exp, axis=3), slot_rows, precision=highest)
    row_lse = row_top + jnp.log(near_total + slot_total)
    near_weights = jnp.exp(near_scores - row_lse[:, :, :, None]).astype(jnp.bfloat16)
    slot_lse = jnp.take(row_lse, recv_block, axis=1)
    slot_weights = jnp.exp(slot_scores - slot_lse[:, :, :, None]).astype(jnp.bfloat16)
    near_out = jnp.einsum(
        "hnqk,nkhe->nqhe", near_weights, band_values, preferred_element_type=jnp.float32
    ).reshape(head_shape)
    slot_out = jnp.einsum(
        "hnqk,nkhe->nqhe", slot_weights, slot_value, preferred_element_type=jnp.float32
    )
    slot_back = jnp.einsum("ni,nqhe->iqhe", slot_rows, slot_out, precision=highest).reshape(
        head_shape
    )
    attended = (near_out + slot_back).astype(jnp.bfloat16)
    global_heads = global_query.reshape(tile_shape)
    global_grads = global_grad.reshape(tile_shape)
    global_mask = lax.dynamic_slice_in_dim(pattern[0], own_index * per_dev, per_dev, 0) > 0
    global_scores = (
        jnp.einsum("qhe,khe->hqk", global_heads, key_heads, preferred_element_type=jnp.float32)
        * score_scale
    )
    global_scores = global_scores.reshape(head_count, block_rows, per_dev, block_rows)
    global_scores = jnp.where(global_mask[None, None, :, None], global_scores, big_negative)
    local_top = jnp.max(global_scores, axis=(2, 3))
    global_top = lax.pmax(local_top, "seq")
    global_total = lax.psum(
        jnp.sum(jnp.exp(global_scores - global_top[:, :, None, None]), axis=(2, 3)), "seq"
    )
    global_lse = global_top + jnp.log(global_total)
    global_weights = (
        jnp.exp(global_scores - global_lse[:, :, None, None])
        .astype(jnp.bfloat16)
        .reshape(head_count, block_rows, frames)
    )
    global_acc = jnp.einsum(
        "hqk,khe->qhe", global_weights, value_heads, preferred_element_type=jnp.float32
    )
    global_out = lax.psum(global_acc, "seq").astype(jnp.bfloat16)
    is_first = own_index == 0
    attended_blocks = attended.reshape(block_shape)
    attended_blocks = attended_blocks.at[0].set(jnp.where(is_first, global_out, attended_blocks[0]))
    attended = attended_blocks.reshape(head_shape)
    row_delta = jnp.sum(grad_heads.astype(jnp.float32) * attended.astype(jnp.float32), axis=2).T
    global_delta = jnp.sum(
        global_grads.astype(jnp.float32) * global_out.astype(jnp.float32), axis=2
    ).T
    block_delta = row_delta.reshape(head_count, per_dev, block_rows)
    near_kept = near_weights * row_live.astype(jnp.bfloat16)[None, :, None, None]
    near_gw = jnp.einsum(
        "nqhe,nkhe->hnqk", grad_blocks, band_values, preferred_element_type=jnp.float32
    )
    near_gs = (near_kept.astype(jnp.float32) * (near_gw - block_delta[:, :, :, None])).astype(
        jnp.bfloat16
    )
    near_dq = jnp.einsum(
        "hnqk,nkhe->nqhe", near_gs, band_keys, preferred_element_type=jnp.float32
    ).reshape(head_shape)
    band_dk = jnp.einsum(
        "hnqk,nqhe->nkhe", near_gs, query_blocks, preferred_element_type=jnp.float32
    )
    band_dv = jnp.einsum(
        "hnqk,nqhe->nkhe", near_kept, grad_blocks, preferred_element_type=jnp.float32
    )
    near_dk = band_return(band_dk, per_dev, block_rows)
    near_dv = band_return(band_dv, per_dev, block_rows)
    slot_grad = jnp.take(grad_blocks, recv_block, axis=0)
    slot_delta = jnp.take(block_delta, recv_block, axis=1)
    slot_gw = jnp.einsum(
        "nqhe,nkhe->hnqk", slot_grad, slot_value, preferred_element_type=jnp.float32
    )
    slot_gs = (slot_weights.astype(jnp.float32) * (slot_gw - slot_delta[:, :, :, None])).astype(
        jnp.bfloat16
    )
    slot_dq = jnp.einsum("hnqk,nkhe->nqhe", slot_gs, slot_key, preferred_element_type=jnp.float32)
    query_sum = near_dq + jnp.einsum(
        "ni,nqhe->iqhe", slot_rows, slot_dq, precision=highest
    ).reshape(head_shape)
    part_dk = jnp.einsum("hnqk,nqhe->nkhe", slot_gs, slot_query, preferred_element_type=jnp.float32)
    part_dv = jnp.einsum(
        "hnqk,nqhe->nkhe", slot_weights, slot_grad, preferred_element_type=jnp.float32
    )
    remote_dk, remote_dv = (
        lax.all_to_all(part_dk, "seq", split_axis=0, concat_axis=0, tiled=True),
        lax.all_to_all(part_dv, "seq", split_axis=0, concat_axis=0, tiled=True),
    )
    remote_key = jnp.einsum("ni,nkhe->ikhe", give_rows, remote_dk, precision=highest).reshape(
        head_shape
    )
    remote_value = jnp.einsum("ni,nkhe->ikhe", give_rows, remote_dv, precision=highest).reshape(
        head_shape
    )
    global_gw = jnp.einsum(
        "qhe,khe->hqk", global_grads, value_heads, preferred_element_type=jnp.float32
    )
    global_gs = (
        global_weights.astype(jnp.float32) * (global_gw - global_delta[:, :, None])
    ).astype(jnp.bfloat16)
    global_dq_part = jnp.einsum(
        "hqk,khe->qhe", global_gs, key_heads, preferred_element_type=jnp.float32
    )
    global_dk_own = jnp.einsum(
        "hqk,qhe->khe", global_gs, global_heads, preferred_element_type=jnp.float32
    )
    global_dv_own = jnp.einsum(
        "hqk,qhe->khe", global_weights, global_grads, preferred_element_type=jnp.float32
    )
    summed_dq, summed_dk, summed_dv = lax.psum(
        (global_dq_part, near_dk[-block_rows:], near_dv[-block_rows:]), "seq"
    )
    right_edge = block_rows + frames
    from_right = passed_along(
        jnp.stack((near_dk[:block_rows], near_dv[:block_rows])).astype(jnp.bfloat16), "seq", -1
    ).astype(jnp.float32)
    from_left = passed_along(
        jnp.stack(
            (
                near_dk[right_edge : right_edge + block_rows],
                near_dv[right_edge : right_edge + block_rows],
            )
        ),
        "seq",
        1,
    )
    key_sum = near_dk[block_rows:right_edge] + global_dk_own + remote_key
    key_sum = key_sum.at[:block_rows].add(from_left[0] + jnp.where(is_first, summed_dk, 0.0))
    key_sum = key_sum.at[frames - block_rows :].add(from_right[0])
    value_sum = near_dv[block_rows:right_edge] + global_dv_own + remote_value
    value_sum = value_sum.at[:block_rows].add(from_left[1] + jnp.where(is_first, summed_dv, 0.0))
    value_sum = value_sum.at[frames - block_rows :].add(from_right[1])
    query_sum = query_sum.at[:block_rows].set(
        jnp.where(is_first, summed_dq, query_sum[:block_rows])
    )
    flat = (frames, width_dev)
    query_result = (query_sum * score_scale).astype(jnp.bfloat16).reshape(flat)
    key_result = (key_sum * score_scale).astype(jnp.bfloat16).reshape(flat)
    value_result = value_sum.astype(jnp.bfloat16).reshape(flat)
    results = (
        lax.all_to_all(attended.reshape(flat), "head", split_axis=0, concat_axis=1, tiled=True),
        lax.all_to_all(query_result, "head", split_axis=0, concat_axis=1, tiled=True),
        lax.all_to_all(key_result, "head", split_axis=0, concat_axis=1, tiled=True),
        lax.all_to_all(value_result, "head", split_axis=0, concat_axis=1, tiled=True),
    )
    return (results[0], results[1], results[2], results[3])


def solution(mesh):
    in_specs = (
        P(("seq", "head"), None),
        P(("seq", "head"), None),
        P(("seq", "head"), None),
        P(("seq", "head"), None),
        P(),
    )
    out_specs = (
        P(("seq", "head"), None),
        P(("seq", "head"), None),
        P(("seq", "head"), None),
        P(("seq", "head"), None),
    )
    return jax.shard_map(body, mesh=mesh, in_specs=in_specs, out_specs=out_specs, check_vma=False)
```

profile of v0, /device:TPU:32, one launch (start us, length us, event | category | flops | bytes accessed | tf_op | source)
XLA Modules:
  0.0 1104.4 jit_solution(2267911232125624621)
XLA Ops:
  16.7 12.5 %all-to-all-done.6 = bf16[256,4,512]{0,2,1:T(8,128)(2,1)S(1)} async-done(((bf16[256,4,512]{0,2,1:T(8,128)(2,1)}), bf16[256,4,512]{0,2,1:T(8,128)(2,1)S(1)}, u32[]{:S(2)}, u32[]{:S(2)}) %all-to-all-start.6) | async-done | bytes 1048608 | tf_op jit(solution)/shard_map/all_to_all | solution.py:86
  35.5 11.4 %all-to-all-done.2 = bf16[256,4,512]{0,2,1:T(8,128)(2,1)S(1)} async-done(((bf16[256,4,512]{0,2,1:T(8,128)(2,1)}), bf16[256,4,512]{0,2,1:T(8,128)(2,1)S(1)}, u32[]{:S(2)}, u32[]{:S(2)}) %all-to-all-start.2) | async-done | bytes 1048608 | tf_op jit(solution)/shard_map/all_to_all | solution.py:83
  55.3 9.2 all-to-all-done
  101.7 8.0 all-to-all-start.3
  112.2 10.5 broadcast_select_fusion
  191.1 88.9 %all-reduce.15.cloned.1.call-done = (bf16[128,4,128]{0,2,1:T(8,128)(2,1)}, bf16[128,4,128]{0,2,1:T(8,128)(2,1)}, bf16[128,4,128]{2,0,1:T(8,128)(2,1)}, bf16[128,4,128]{2,0,1:T(8,128)(2,1)}) async-done(((bf16[128,4,128]{0,2,1:T(8,128)(2,1)}, bf16[128,4,128]{0,2,1:T(8,128)(2,1)}, bf16[128,4,128]{2,0,1:T(8,128)(2,1)}, bf16[128,4,128]{2,0,1:T(8,128)(2,1)}), (bf16[128,4,128]{0,2,1:T(8,128)(2,1)}, ...) | async-done | bytes 524304 | tf_op jit(solution)/shard_map/psum | solution.py:16
  284.6 7.5 copy.449
  302.2 7.6 copy.438
  311.6 54.8 %pmax.7 = f32[4,128]{1,0:T(4,128)S(1)} all-reduce(f32[4,128]{1,0:T(4,128)S(1)} %get-tuple-element.135), channel_id=1, replica_groups=mesh['seq'=32,'head'=4] {'seq'}, use_global_device_ids=true, to_apply=%region_13.16 | all-reduce | flops 512 | bytes 4096 | tf_op jit(solution)/shard_map/pmax | solution.py:203
  368.4 57.3 %psum.66 = f32[4,128]{1,0:T(4,128)S(1)} all-reduce(f32[4,128]{1,0:T(4,128)S(1)} %exponential_reduce_fusion.1), channel_id=1, replica_groups=mesh['seq'=32,'head'=4] {'seq'}, use_global_device_ids=true, to_apply=%region_15.18 | all-reduce | flops 512 | bytes 4096 | tf_op jit(solution)/shard_map/psum | solution.py:204
  429.9 125.6 %all-reduce.16 = bf16[128,4,128]{2,0,1:T(8,128)(2,1)S(1)} all-reduce(f32[128,4,128]{2,0,1:T(8,128)} %convolution_bitcast_fusion.1), channel_id=1, replica_groups=mesh['seq'=32,'head'=4] {'seq'}, use_global_device_ids=true, to_apply=%region_16.19 | all-reduce | flops 65536 | bytes 393216 | tf_op jit(solution)/shard_map/psum | solution.py:216
  561.4 23.5 %all-to-all-start.4 = ((bf16[32,128,4,128]{1,3,2,0:T(8,128)(2,1)}), bf16[32,128,4,128]{1,3,2,0:T(8,128)(2,1)}, u32[]{:S(2)}, u32[]{:S(2)}) async-start(bf16[32,128,4,128]{1,3,2,0:T(8,128)(2,1)} %broadcast_select_fusion.2), calls=%async_computation.4 | async-start | bytes 8388608 | tf_op jit(solution)/shard_map/all_to_all | solution.py:130
  584.9 9.7 fusion.5
  611.0 7.1 broadcast_multiply_fusion
  618.1 17.1 %all-to-all-done.4 = bf16[32,128,4,128]{1,3,2,0:T(8,128)(2,1)} async-done(((bf16[32,128,4,128]{1,3,2,0:T(8,128)(2,1)}), bf16[32,128,4,128]{1,3,2,0:T(8,128)(2,1)}, u32[]{:S(2)}, u32[]{:S(2)}) %all-to-all-start.4) | async-done | bytes 4194336 | tf_op jit(solution)/shard_map/all_to_all | solution.py:130
  635.2 8.0 fusion.30
  643.2 10.4 copy.467
  668.3 9.3 multiply_convert_fusion
  677.5 8.6 fusion.36
  686.1 7.9 all-to-all-start.8
  694.0 9.8 fusion.41
  703.9 91.1 %all-to-all-done.8 = f32[32,128,4,128]{1,3,2,0:T(8,128)} async-done(((f32[32,128,4,128]{1,3,2,0:T(8,128)}), f32[32,128,4,128]{1,3,2,0:T(8,128)}, u32[]{:S(2)}, u32[]{:S(2)}) %all-to-all-start.8) | async-done | bytes 8388640 | tf_op jit(solution)/shard_map/all_to_all | solution.py:261
  794.9 10.1 all-to-all-start.10
  805.1 7.5 copy.560
  812.7 7.5 copy.559
  850.0 7.0 fusion.33
  857.0 10.7 copy.495
  883.9 19.3 %collective-permute-done.3 = bf16[2,128,4,128]{3,1,2,0:T(8,128)(2,1)} collective-permute-done((bf16[2,128,4,128]{3,1,2,0:T(8,128)(2,1)}, bf16[2,128,4,128]{3,1,2,0:T(8,128)(2,1)}, u32[]{:S(2)}, u32[]{:S(2)}) %collective-permute-start.3) | collective-permute-done | bytes 262176 | tf_op jit(solution)/shard_map/ppermute | solution.py:35
  905.0 89.1 %all-reduce.13.cloned.1.call-done = (f32[128,4,128]{2,0,1:T(8,128)}, f32[128,4,128]{2,0,1:T(8,128)}, f32[128,4,128]{2,0,1:T(8,128)}) async-done(((f32[128,4,128]{2,0,1:T(8,128)}, f32[128,4,128]{2,0,1:T(8,128)}, f32[128,4,128]{2,0,1:T(8,128)}), (f32[128,4,128]{2,0,1:T(8,128)}, f32[128,4,128]{2,0,1:T(8,128)}, f32[128,4,128]{2,0,1:T(8,128)})) %all-reduce.13.cloned.1.call-update) | async-done | bytes 786448 | tf_op jit(solution)/shard_map/psum | solution.py:285
  998.7 10.4 copy.515
  1021.3 10.4 copy.529
  1067.1 11.8 %all-to-all-done.9 = bf16[4,256,512]{2,1,0:T(8,128)(2,1)} async-done(((bf16[4,256,512]{2,1,0:T(8,128)(2,1)}), bf16[4,256,512]{2,1,0:T(8,128)(2,1)}, u32[]{:S(2)}, u32[]{:S(2)}) %all-to-all-start.9) | async-done | bytes 1048608 | tf_op jit(solution)/shard_map/all_to_all | solution.py:318
  (289 shorter events, 309.5 us)
Async XLA Ops:
  7.2 8.0 copy-start.29
  7.2 9.4 copy-start.37
  7.2 25.8 %copy-start.30 = (bf16[256,2048]{1,0:T(8,128)(2,1)S(1)}, bf16[256,2048]{1,0:T(8,128)(2,1)}, u32[]{:S(2)}) copy-start(bf16[256,2048]{1,0:T(8,128)(2,1)} %param.22) | copy-start | bytes 3145732
  9.6 19.6 %all-to-all-start.6 = ((bf16[256,4,512]{0,2,1:T(8,128)(2,1)}), bf16[256,4,512]{0,2,1:T(8,128)(2,1)S(1)}, u32[]{:S(2)}, u32[]{:S(2)}) async-start(bf16[256,4,512]{0,2,1:T(8,128)(2,1)} %bitcast.39), calls=%async_computation.6 | async-start | bytes 2097152 | tf_op jit(solution)/shard_map/all_to_all | solution.py:86
  29.2 40.6 %copy-start.13 = (bf16[256,4,512]{0,2,1:T(8,128)(2,1)}, bf16[256,4,512]{0,2,1:T(8,128)(2,1)S(1)}, u32[]{:S(2)}) copy-start(bf16[256,4,512]{0,2,1:T(8,128)(2,1)S(1)} %all-to-all-done.6) | copy-start | bytes 3145732
  29.2 17.7 %all-to-all-start.2 = ((bf16[256,4,512]{0,2,1:T(8,128)(2,1)}), bf16[256,4,512]{0,2,1:T(8,128)(2,1)S(1)}, u32[]{:S(2)}, u32[]{:S(2)}) async-start(bf16[256,4,512]{0,2,1:T(8,128)(2,1)} %bitcast.17), calls=%async_computation.2 | async-start | bytes 2097152 | tf_op jit(solution)/shard_map/all_to_all | solution.py:83
  32.7 21.9 %slice-start.3 = ((s32[256,256]{1,0:T(8,128)}), s32[1,256]{1,0:T(1,128)S(1)}, s32[]{:S(2)}) async-start(s32[256,256]{1,0:T(8,128)} %param.25), calls=%async_computation.17 | async-start | bytes 2048 | tf_op jit(solution)/shard_map/slice | solution.py:195
  47.8 16.8 %all-to-all-start = ((bf16[256,4,512]{0,2,1:T(8,128)(2,1)}), bf16[256,4,512]{0,2,1:T(8,128)(2,1)S(1)}, u32[]{:S(2)}, u32[]{:S(2)}) async-start(bf16[256,4,512]{0,2,1:T(8,128)(2,1)} %bitcast.253), calls=%async_computation | async-start | bytes 2097152 | tf_op jit(solution)/shard_map/all_to_all | solution.py:84
  64.6 10.1 copy-start.14
  64.6 37.1 %all-to-all-start.1 = ((bf16[256,4,512]{0,2,1:T(8,128)(2,1)}), bf16[256,4,512]{0,2,1:T(8,128)(2,1)}, u32[]{:S(2)}, u32[]{:S(2)}) async-start(bf16[256,4,512]{0,2,1:T(8,128)(2,1)} %bitcast.254), calls=%async_computation.1 | async-start | bytes 2097152 | tf_op jit(solution)/shard_map/all_to_all | solution.py:85
  69.6 23.0 %copy-start.35 = (s32[1024]{0:T(1024)}, s32[1024]{0:T(1024)S(1)}, u32[]{:S(2)}) copy-start(s32[1024]{0:T(1024)S(1)} %pad_clamp_fusion) | copy-start | bytes 12292
  101.7 459.7 %all-to-all-start.3 = ((bf16[32,128,4,128]{3,1,2,0:T(8,128)(2,1)}), bf16[32,128,4,128]{3,1,2,0:T(8,128)(2,1)}, u32[]{:S(2)}, u32[]{:S(2)}) async-start(bf16[32,128,4,128]{3,1,2,0:T(8,128)(2,1)} %broadcast_select_fusion.3), calls=%async_computation.3 | async-start | bytes 8388608 | tf_op jit(solution)/shard_map/all_to_all | solution.py:127
  109.7 170.3 %all-reduce.15.cloned.1.call-start = ((), (), s32[]{:S(2)}) async-start(), calls=%async_computation.13 | async-start | bytes 1048576 | tf_op jit(solution)/shard_map/psum | solution.py:16
  112.2 13.1 %copy-start.15 = (bf16[256,4,512]{0,2,1:T(8,128)(2,1)S(1)}, bf16[256,4,512]{0,2,1:T(8,128)(2,1)}, u32[]{:S(2)}) copy-start(bf16[256,4,512]{0,2,1:T(8,128)(2,1)} %copy-done.14) | copy-start | bytes 3145732
  142.9 39.1 %collective-permute-start = (bf16[2,128,512]{2,1,0:T(8,128)(2,1)}, bf16[2,128,512]{2,1,0:T(8,128)(2,1)}, u32[]{:S(2)}, u32[]{:S(2)}) collective-permute-start(bf16[2,128,512]{2,1,0:T(8,128)(2,1)} %get-tuple-element.123), channel_id=1, source_target_pairs={{0,4},{4,8},{8,12},{12,16},{16,20},{20,24},{24,28},{28,32},{32,36}... | collective-permute-start | bytes 786440 | tf_op jit(solution)/shard_map/ppermute | solution.py:24
  144.9 37.0 %collective-permute-start.1 = (bf16[2,128,512]{2,1,0:T(8,128)(2,1)S(1)}, bf16[2,128,512]{2,1,0:T(8,128)(2,1)}, u32[]{:S(2)}, u32[]{:S(2)}) collective-permute-start(bf16[2,128,512]{2,1,0:T(8,128)(2,1)S(1)} %get-tuple-element.124), channel_id=1, source_target_pairs={{4,0},{8,4},{12,8},{16,12},{20,16},{24,20},{28,24},{32,28},{36,32}... | collective-permute-start | bytes 786440 | tf_op jit(solution)/shard_map/ppermute | solution.py:27
  302.1 7.6 copy-start.36
  311.6 117.1 %copy-start.27 = (bf16[1024,4,128]{2,1,0:T(4,128)(2,1)S(1)}, bf16[1024,4,128]{2,1,0:T(4,128)(2,1)}, u32[]{:S(2)}) copy-start(bf16[1024,4,128]{2,1,0:T(4,128)(2,1)} %reshape.553) | copy-start | bytes 3145732
  561.4 73.8 %all-to-all-start.4 = ((bf16[32,128,4,128]{1,3,2,0:T(8,128)(2,1)}), bf16[32,128,4,128]{1,3,2,0:T(8,128)(2,1)}, u32[]{:S(2)}, u32[]{:S(2)}) async-start(bf16[32,128,4,128]{1,3,2,0:T(8,128)(2,1)} %broadcast_select_fusion.2), calls=%async_computation.4 | async-start | bytes 8388608 | tf_op jit(solution)/shard_map/all_to_all | solution.py:130
  584.9 9.8 copy-start.34
  668.3 9.3 copy-start.6
  686.1 108.8 %all-to-all-start.8 = ((f32[32,128,4,128]{1,3,2,0:T(8,128)}), f32[32,128,4,128]{1,3,2,0:T(8,128)}, u32[]{:S(2)}, u32[]{:S(2)}) async-start(f32[32,128,4,128]{1,3,2,0:T(8,128)} %fusion.36), calls=%async_computation.8 | async-start | bytes 16777216 | tf_op jit(solution)/shard_map/all_to_all | solution.py:261
  794.9 221.9 %all-to-all-start.10 = ((f32[32,128,4,128]{1,3,2,0:T(8,128)}), f32[32,128,4,128]{1,3,2,0:T(8,128)}, u32[]{:S(2)}, u32[]{:S(2)}) async-start(f32[32,128,4,128]{1,3,2,0:T(8,128)} %fusion.41), calls=%async_computation.10 | async-start | bytes 16777216 | tf_op jit(solution)/shard_map/all_to_all | solution.py:262
  805.1 189.0 %all-reduce.13.cloned.1.call-start = ((), (), s32[]{:S(2)}) async-start(), calls=%async_computation.12 | async-start | bytes 1572864 | tf_op jit(solution)/shard_map/psum | solution.py:285
  841.1 8.8 copy-start.9
  842.6 60.6 %collective-permute-start.3 = (bf16[2,128,4,128]{3,1,2,0:T(8,128)(2,1)}, bf16[2,128,4,128]{3,1,2,0:T(8,128)(2,1)}, u32[]{:S(2)}, u32[]{:S(2)}) collective-permute-start(bf16[2,128,4,128]{3,1,2,0:T(8,128)(2,1)} %pad_maximum_fusion.11), channel_id=1, source_target_pairs={{4,0},{8,4},{12,8},{16,12},{20,16},{24,20},{28,24},{32,28},{36,32}... | collective-permute-start | bytes 786440 | tf_op jit(solution)/shard_map/ppermute | solution.py:35
  848.0 197.7 %collective-permute-start.2 = (f32[2,128,4,128]{3,1,2,0:T(8,128)}, f32[2,128,4,128]{3,1,2,0:T(8,128)}, u32[]{:S(2)}, u32[]{:S(2)}) collective-permute-start(f32[2,128,4,128]{3,1,2,0:T(8,128)} %pad_maximum_fusion.8), channel_id=1, source_target_pairs={{0,4},{4,8},{8,12},{12,16},{16,20},{20,24},{24,28},{28,32},{32,36}... | collective-permute-start | bytes 1572872 | tf_op jit(solution)/shard_map/ppermute | solution.py:35
  1016.9 24.1 %all-to-all-start.5 = ((bf16[4,256,512]{2,1,0:T(8,128)(2,1)}), bf16[4,256,512]{2,1,0:T(8,128)(2,1)S(1)}, u32[]{:S(2)}, u32[]{:S(2)}) async-start(bf16[4,256,512]{2,1,0:T(8,128)(2,1)} %all_to_all.138), calls=%async_computation.5 | async-start | bytes 2097152 | tf_op jit(solution)/shard_map/all_to_all | solution.py:316
  1040.9 19.8 %all-to-all-start.7 = ((bf16[4,256,512]{2,1,0:T(8,128)(2,1)}), bf16[4,256,512]{2,1,0:T(8,128)(2,1)}, u32[]{:S(2)}, u32[]{:S(2)}) async-start(bf16[4,256,512]{2,1,0:T(8,128)(2,1)} %all_to_all.146), calls=%async_computation.7 | async-start | bytes 2097152 | tf_op jit(solution)/shard_map/all_to_all | solution.py:317
  1049.7 15.2 %copy-start.10 = (f32[1024,4,128]{2,0,1:T(8,128)S(1)}, f32[1024,4,128]{2,0,1:T(8,128)}, u32[]{:S(2)}) copy-start(f32[1024,4,128]{2,0,1:T(8,128)} %get-tuple-element.125) | copy-start | bytes 6291460
  1060.7 18.2 %all-to-all-start.9 = ((bf16[4,256,512]{2,1,0:T(8,128)(2,1)}), bf16[4,256,512]{2,1,0:T(8,128)(2,1)}, u32[]{:S(2)}, u32[]{:S(2)}) async-start(bf16[4,256,512]{2,1,0:T(8,128)(2,1)} %all_to_all.151), calls=%async_computation.9 | async-start | bytes 2097152 | tf_op jit(solution)/shard_map/all_to_all | solution.py:318
  1078.9 16.5 %all-to-all-start.11 = ((bf16[4,256,512]{2,1,0:T(8,128)(2,1)}), bf16[4,256,512]{2,1,0:T(8,128)(2,1)S(1)}, u32[]{:S(2)}, u32[]{:S(2)}) async-start(bf16[4,256,512]{2,1,0:T(8,128)(2,1)} %all_to_all.156), calls=%async_computation.11 | async-start | bytes 2097152 | tf_op jit(solution)/shard_map/all_to_all | solution.py:319
  (29 other events, 128.8 us)
Sparse Core Ops, SparseCore 0:
  177.3 102.5 all-reduce.14
  867.9 126.2 all-reduce.12
where the time goes:
time: 1120 us; the launch traced here: 1100 us
  waiting for transfers between devices  363 us (32%)
  blocking collectives  238 us (21%)
  local copies, waits for them, and re-layouts  209 us (19%)
  matrix products  102 us (9%)
  starting transfers between devices  96.9 us (9%)
  other arithmetic  80.2 us (7%)
  between operations  15.2 us (1%)
    psum x1, blocking collectives, body(): global_out = lax.psum(global_acc, 'seq').astype(jnp.bfloat16)  126 us
    all_to_all x1, waiting for transfers between devices, body(): lax.all_to_all(part_dk, 'seq', split_axis=0, concat_axis=0, tiled=True)  91.1 us
    psum x1, waiting for transfers between devices, body(): lax.psum((global_dq_part, near_dk[-block_rows:], near_dv[-block_rows:]),...  89.1 us
    psum x1, waiting for transfers between devices, spread(): return lax.psum(block, axis)  88.9 us
    psum x1, blocking collectives, body(): lax.psum(jnp.sum(jnp.exp(global_scores - global_top[:, :, None, None]), a...  57.3 us
    pmax x1, blocking collectives, body(): global_top = lax.pmax(local_top, 'seq')  54.8 us
    another operation x16, local copies, waits for them, and re-layouts, band_stack(): jnp.stack((padded_blocks[0:per_dev], padded_blocks[1:per_dev + 1], padded...  37.9 us
    all_to_all x1, starting transfers between devices, body(): lax.all_to_all(jnp.take(value_blocks, send_block, axis=0), 'seq', split_a...  23.5 us
  transfers between devices with their start and end apart: 18, of which 11 were waited for; matrix products, arithmetic and copies ran while one was open for 29% of the time, Pallas kernels for 0%

commit v1 on v0

v1 whole, which is shorter than its diff:
```python
import functools

import jax
import jax.numpy as jnp
from jax import lax
from jax.experimental import pallas as pl
from jax.experimental.pallas import tpu as pltpu
from jax.sharding import PartitionSpec as P

HEAD_DIM = 128
BLOCK = 128
SCALE = HEAD_DIM ** (-0.5)
NEG = -1e30
MESH = pl.DeviceIdType.MESH
ANY = pl.BlockSpec(memory_space=pl.ANY)
SMEM = pl.BlockSpec(memory_space=pltpu.SMEM)
F32, BF16 = jnp.float32, jnp.bfloat16


def nt(a, b):
    return lax.dot_general(a, b, (((1,), (1,)), ((), ())), preferred_element_type=F32)


def tn(a, b):
    return lax.dot_general(a, b, (((0,), (0,)), ((), ())), preferred_element_type=F32)


def nn(a, b):
    return jnp.dot(a, b, preferred_element_type=F32)


def barrier_with(axis, me, count):
    sem = pltpu.get_barrier_semaphore()

    def greet(step, carry):
        pl.semaphore_signal(
            sem, inc=1, device_id={axis: lax.rem(me + step, count)}, device_id_type=MESH
        )
        return carry

    lax.fori_loop(1, count, greet, 0)
    pl.semaphore_wait(sem, count - 1)


def heads_in_kernel(count, narr, *refs):
    xs, outs = refs[:narr], refs[narr : 2 * narr]
    send, recv, local = refs[2 * narr :]
    me = lax.axis_index("head")
    width = xs[0].shape[1] // count
    barrier_with("head", me, count)
    copies = []
    for a in range(narr):
        for step in range(1, count):
            peer = lax.rem(me + step, count)
            copies.append(
                pltpu.make_async_remote_copy(
                    src_ref=xs[a].at[:, pl.ds(pl.multiple_of(peer * width, width), width)],
                    dst_ref=outs[a].at[me],
                    send_sem=send.at[a, step],
                    recv_sem=recv.at[a, step],
                    device_id={"head": peer},
                    device_id_type=MESH,
                )
            )
            copies[-1].start()
        copies.append(
            pltpu.make_async_copy(
                xs[a].at[:, pl.ds(pl.multiple_of(me * width, width), width)],
                outs[a].at[me],
                local.at[a],
            )
        )
        copies[-1].start()
    for copy in copies:
        copy.wait()


def heads_in(xs, ident):
    count, narr = lax.axis_size("head"), len(xs)
    rows, width = xs[0].shape
    outs = pl.pallas_call(
        functools.partial(heads_in_kernel, count, narr),
        out_shape=[jax.ShapeDtypeStruct((count, rows, width // count), x.dtype) for x in xs],
        in_specs=[ANY] * narr,
        out_specs=[ANY] * narr,
        scratch_shapes=[
            pltpu.SemaphoreType.DMA((narr, count)),
            pltpu.SemaphoreType.DMA((narr, count)),
            pltpu.SemaphoreType.DMA((narr,)),
        ],
        compiler_params=pltpu.CompilerParams(collective_id=ident, has_side_effects=True),
        name="heads_in",
    )(*xs)
    return [o.reshape(count * rows, width // count) for o in outs]


def heads_out_kernel(count, narr, *refs):
    xs, outs = refs[:narr], refs[narr : 2 * narr]
    send, recv, local = refs[2 * narr :]
    me = lax.axis_index("head")
    width = xs[0].shape[1]
    rows = xs[0].shape[0] // count
    barrier_with("head", me, count)
    mine = pl.ds(pl.multiple_of(me * width, width), width)
    copies = []
    for a in range(narr):
        for step in range(1, count):
            peer = lax.rem(me + step, count)
            copies.append(
                pltpu.make_async_remote_copy(
                    src_ref=xs[a].at[pl.ds(pl.multiple_of(peer * rows, rows), rows)],
                    dst_ref=outs[a].at[:, mine],
                    send_sem=send.at[a, step],
                    recv_sem=recv.at[a, step],
                    device_id={"head": peer},
                    device_id_type=MESH,
                )
            )
            copies[-1].start()
        copies.append(
            pltpu.make_async_copy(
                xs[a].at[pl.ds(pl.multiple_of(me * rows, rows), rows)],
                outs[a].at[:, mine],
                local.at[a],
            )
        )
        copies[-1].start()
    for copy in copies:
        copy.wait()


def heads_out(xs, ident):
    count, narr = lax.axis_size("head"), len(xs)
    frames, width = xs[0].shape
    return pl.pallas_call(
        functools.partial(heads_out_kernel, count, narr),
        out_shape=[jax.ShapeDtypeStruct((frames // count, width * count), x.dtype) for x in xs],
        in_specs=[ANY] * narr,
        out_specs=[ANY] * narr,
        scratch_shapes=[
            pltpu.SemaphoreType.DMA((narr, count)),
            pltpu.SemaphoreType.DMA((narr, count)),
            pltpu.SemaphoreType.DMA((narr,)),
        ],
        compiler_params=pltpu.CompilerParams(collective_id=ident, has_side_effects=True),
        name="heads_out",
    )(*xs)


def edges_kernel(count, q, k, v, g, edge, first, send, recv, scatter_send, scatter_recv, local, near):
    me = lax.axis_index("seq")
    arrays = (q, k, v, g)
    frames = q.shape[0]
    barrier_with("seq", me, count)
    right, left = lax.rem(me + 1, count), lax.rem(me + count - 1, count)
    copies = []
    for a, x in enumerate((k, v)):
        for side, (peer, rows) in enumerate(
            ((right, pl.ds(frames - BLOCK, BLOCK)), (left, pl.ds(0, BLOCK)))
        ):
            copies.append(
                pltpu.make_async_remote_copy(
                    src_ref=x.at[rows],
                    dst_ref=edge.at[a, side],
                    send_sem=near.at[0, a, side],
                    recv_sem=near.at[1, a, side],
                    device_id={"seq": peer},
                    device_id_type=MESH,
                )
            )
            copies[-1].start()

    def piece(a, unit):
        rows = pl.multiple_of(lax.rem(unit, 8) * 16, 16)
        columns = pl.multiple_of((unit // 8) * HEAD_DIM, HEAD_DIM)
        return arrays[a].at[pl.ds(rows, 16), pl.ds(columns, HEAD_DIM)]

    def scatter_copy(a, unit):
        return pltpu.make_async_remote_copy(
            src_ref=piece(a, unit),
            dst_ref=first.at[a, unit],
            send_sem=scatter_send.at[a, unit],
            recv_sem=scatter_recv.at[a],
            device_id={"seq": unit},
            device_id_type=MESH,
        )

    @pl.when(me == 0)
    def _():
        def start(unit, carry):
            for a in range(4):
                scatter_copy(a, unit).start()
            return carry

        lax.fori_loop(1, count, start, 0)
        for a in range(4):
            own = pltpu.make_async_copy(piece(a, 0), first.at[a, 0], local.at[a])
            own.start()
        for a in range(4):
            pltpu.make_async_copy(piece(a, 0), first.at[a, 0], local.at[a]).wait()

    @pl.when(me > 0)
    def _():
        for a in range(4):
            pltpu.make_async_copy(first.at[a, me], first.at[a, me], scatter_recv.at[a]).wait()

    def pass_copy(step, slot):
        peer = lax.rem(me + step, count)
        return pltpu.make_async_remote_copy(
            src_ref=first.at[:, me],
            dst_ref=first.at[:, me],
            send_sem=send.at[step],
            recv_sem=recv.at[step],
            device_id={"seq": peer},
            device_id_type=MESH,
        )

    def start_pass(step, carry):
        pass_copy(step, me).start()
        return carry

    def wait_pass(step, carry):
        source = lax.rem(me + count - step, count)
        landed = first.at[:, source]
        pltpu.make_async_copy(landed, landed, recv.at[step]).wait()
        mine = first.at[:, me]
        pltpu.make_async_copy(mine, mine, send.at[step]).wait()
        return carry

    lax.fori_loop(1, count, start_pass, 0)
    lax.fori_loop(1, count, wait_pass, 0)

    @pl.when(me == 0)
    def _():
        def done(unit, carry):
            for a in range(4):
                pltpu.make_async_copy(piece(a, unit), piece(a, unit), scatter_send.at[a, unit]).wait()
            return carry

        lax.fori_loop(1, count, done, 0)

    for copy in copies:
        copy.wait()


def edges(q, k, v, g, ident):
    count = lax.axis_size("seq")
    width = q.shape[1]
    return pl.pallas_call(
        functools.partial(edges_kernel, count),
        out_shape=[
            jax.ShapeDtypeStruct((2, 2, BLOCK, width), BF16),
            jax.ShapeDtypeStruct((4, count, 16, HEAD_DIM), BF16),
        ],
        in_specs=[ANY] * 4,
        out_specs=[ANY] * 2,
        scratch_shapes=[
            pltpu.SemaphoreType.DMA((count,)),
            pltpu.SemaphoreType.DMA((count,)),
            pltpu.SemaphoreType.DMA((4, count)),
            pltpu.SemaphoreType.DMA((4,)),
            pltpu.SemaphoreType.DMA((4,)),
            pltpu.SemaphoreType.DMA((2, 2, 2)),
        ],
        compiler_params=pltpu.CompilerParams(collective_id=ident, has_side_effects=True),
        name="edges",
    )(q, k, v, g)


def exchange_kernel(count, nall, nsame, nside, *refs):
    ins = refs[: nall + nsame + nside]
    outs = refs[nall + nsame + nside : 2 * (nall + nsame + nside)]
    send, recv, local, near = refs[2 * (nall + nsame + nside) :]
    me = lax.axis_index("seq")
    barrier_with("seq", me, count)
    right, left = lax.rem(me + 1, count), lax.rem(me + count - 1, count)
    far = nall + nsame

    def source(a, peer):
        return ins[a].at[peer] if a < nall else ins[a]

    def copy(a, step):
        peer = lax.rem(me + step, count)
        return pltpu.make_async_remote_copy(
            src_ref=source(a, peer),
            dst_ref=outs[a].at[me],
            send_sem=send.at[a, step],
            recv_sem=recv.at[a, step],
            device_id={"seq": peer},
            device_id_type=MESH,
        )

    def start(step, carry):
        for a in range(far):
            copy(a, step).start()
        return carry

    lax.fori_loop(1, count, start, 0)
    copies = []
    for a in range(far):
        copies.append(pltpu.make_async_copy(source(a, me), outs[a].at[me], local.at[a]))
        copies[-1].start()
    for a in range(nside):
        for side, peer in enumerate((right, left)):
            copies.append(
                pltpu.make_async_remote_copy(
                    src_ref=ins[far + a].at[side],
                    dst_ref=outs[far + a].at[side],
                    send_sem=near.at[0, a, side],
                    recv_sem=near.at[1, a, side],
                    device_id={"seq": peer},
                    device_id_type=MESH,
                )
            )
            copies[-1].start()

    def finish(step, carry):
        for a in range(far):
            landed = outs[a].at[lax.rem(me + count - step, count)]
            pltpu.make_async_copy(landed, landed, recv.at[a, step]).wait()
            sent = source(a, lax.rem(me + step, count))
            pltpu.make_async_copy(sent, sent, send.at[a, step]).wait()
        return carry

    lax.fori_loop(1, count, finish, 0)
    for c in copies:
        c.wait()


def exchange(ident, to_each=(), to_all=(), to_sides=()):
    count = lax.axis_size("seq")
    ins = list(to_each) + list(to_all) + list(to_sides)
    shapes = [x.shape for x in to_each]
    shapes += [(count,) + x.shape for x in to_all]
    shapes += [x.shape for x in to_sides]
    far = len(to_each) + len(to_all)
    return pl.pallas_call(
        functools.partial(exchange_kernel, count, len(to_each), len(to_all), len(to_sides)),
        out_shape=[jax.ShapeDtypeStruct(s, x.dtype) for s, x in zip(shapes, ins)],
        in_specs=[ANY] * len(ins),
        out_specs=[ANY] * len(ins),
        scratch_shapes=[
            pltpu.SemaphoreType.DMA((max(far, 1), count)),
            pltpu.SemaphoreType.DMA((max(far, 1), count)),
            pltpu.SemaphoreType.DMA((max(far, 1),)),
            pltpu.SemaphoreType.DMA((2, max(len(to_sides), 1), 2)),
        ],
        compiler_params=pltpu.CompilerParams(collective_id=ident, has_side_effects=True),
        name="exchange",
    )(*ins)


def pick_kernel(block_of, a, b, out, sem):
    count = out.shape[0]

    def start(slot, carry):
        rows = pl.ds(pl.multiple_of(block_of[slot] * BLOCK, BLOCK), BLOCK)
        pltpu.make_async_copy(a.at[rows], out.at[slot, 0], sem).start()
        pltpu.make_async_copy(b.at[rows], out.at[slot, 1], sem).start()
        return carry

    lax.fori_loop(0, count, start, 0)
    pltpu.make_async_copy(out, out, sem).wait()


def pick(block_of, a, b):
    count = block_of.shape[0]
    return pl.pallas_call(
        pick_kernel,
        out_shape=jax.ShapeDtypeStruct((count, 2, BLOCK, a.shape[1]), a.dtype),
        in_specs=[SMEM] + [pl.BlockSpec(memory_space=pltpu.VMEM)] * 2,
        out_specs=ANY,
        scratch_shapes=[pltpu.SemaphoreType.DMA],
        cost_estimate=pl.CostEstimate(flops=0, bytes_accessed=16 << 20, transcendentals=0),
        name="pick",
    )(block_of, a, b)


def rows_kernel(
    order, off, group, q_in, k_in, v_in, g_in, edge_in, first_in, slot_in, first_out,
    out_ref, dq_ref, dk_ref, dv_ref, dk0_ref, dv0_ref, stat_ref,
    q, k, v, g, slot, kg, vg, near, nearp, link, linkp, top, total, acc, sem,
):
    heads = q.shape[1] // HEAD_DIM
    blocks = q.shape[0] // BLOCK
    frames = q.shape[0]
    own = group[0]
    last = group[1]
    copies = [
        pltpu.make_async_copy(q_in, q, sem.at[0]),
        pltpu.make_async_copy(g_in, g, sem.at[1]),
        pltpu.make_async_copy(k_in, k.at[pl.ds(BLOCK, frames)], sem.at[2]),
        pltpu.make_async_copy(v_in, v.at[pl.ds(BLOCK, frames)], sem.at[3]),
        pltpu.make_async_copy(edge_in.at[0, 0], k.at[pl.ds(0, BLOCK)], sem.at[4]),
        pltpu.make_async_copy(edge_in.at[0, 1], k.at[pl.ds(BLOCK + frames, BLOCK)], sem.at[5]),
        pltpu.make_async_copy(edge_in.at[1, 0], v.at[pl.ds(0, BLOCK)], sem.at[6]),
        pltpu.make_async_copy(edge_in.at[1, 1], v.at[pl.ds(BLOCK + frames, BLOCK)], sem.at[7]),
        pltpu.make_async_copy(first_in.at[1], kg, sem.at[8]),
        pltpu.make_async_copy(first_in.at[2], vg, sem.at[9]),
        pltpu.make_async_copy(slot_in, slot, sem.at[10]),
    ]
    for copy in copies:
        copy.start()
    dk_ref[...] = jnp.zeros_like(dk_ref)
    dv_ref[...] = jnp.zeros_like(dv_ref)
    dk0_ref[...] = jnp.zeros_like(dk0_ref)
    dv0_ref[...] = jnp.zeros_like(dv0_ref)
    for copy in copies:
        copy.wait()
    cols = [slice(h * HEAD_DIM, (h + 1) * HEAD_DIM) for h in range(heads)]
    band = 3 * BLOCK

    def row(i, carry):
        base = pl.multiple_of(i * BLOCK, BLOCK)
        rows = pl.ds(base, BLOCK)
        wide = pl.ds(base, band)
        row_id = own * blocks + i
        begin, end = off[i], off[i + 1]
        column_id = row_id - 1 + lax.broadcasted_iota(jnp.int32, (1, band), 1) // BLOCK
        bias = jnp.where((column_id > 0) & (column_id <= last), 0.0, NEG)
        keep = (row_id > 0).astype(F32)
        for h in range(heads):
            qh = q[rows, cols[h]]
            s = nt(qh, k[wide, cols[h]]) * SCALE + bias
            sg = nt(qh, kg[h]) * SCALE
            near[h, :, :band] = s
            near[h, :, band:] = sg
            top[h] = jnp.maximum(
                jnp.maximum(s[:, :BLOCK], s[:, BLOCK : 2 * BLOCK]),
                jnp.maximum(s[:, 2 * BLOCK :], sg),
            )

        def score(t, c):
            n = order[t]
            for h in range(heads):
                s = nt(q[rows, cols[h]], slot[n, 0, :, cols[h]]) * SCALE
                link[t - begin, h] = s
                top[h] = jnp.maximum(top[h], s)
            return c

        lax.fori_loop(begin, end, score, 0)
        tops = [jnp.max(top[h], axis=1, keepdims=True) for h in range(heads)]
        for h in range(heads):
            e = jnp.exp(near[h] - tops[h])
            total[h] = (e[:, :BLOCK] + e[:, BLOCK : 2 * BLOCK]) + (e[:, 2 * BLOCK : band] + e[:, band:])
            top[h] = jnp.broadcast_to(tops[h], (BLOCK, BLOCK))

        def expo(t, c):
            for h in range(heads):
                total[h] += jnp.exp(link[t - begin, h] - top[h])
            return c

        lax.fori_loop(begin, end, expo, 0)
        sums = [jnp.sum(total[h], axis=1, keepdims=True) for h in range(heads)]
        lses = [tops[h] + jnp.log(sums[h]) for h in range(heads)]
        for h in range(heads):
            top[h] = jnp.broadcast_to(lses[h], (BLOCK, BLOCK))
            w = (jnp.exp(near[h] - lses[h]) * keep).astype(BF16)
            nearp[h] = w
            acc[h] = nn(w[:, :band], v[wide, cols[h]]) + nn(w[:, band:], vg[h])

        def attend(t, c):
            n = order[t]
            for h in range(heads):
                w = jnp.exp(link[t - begin, h] - top[h]).astype(BF16)
                linkp[t - begin, h] = w
                acc[h] += nn(w, slot[n, 1, :, cols[h]])
            return c

        lax.fori_loop(begin, end, attend, 0)
        is_first = row_id == 0
        deltas = []
        for h in range(heads):
            o = jnp.where(is_first, first_out[h], acc[h]).astype(BF16)
            out_ref[rows, cols[h]] = o
            gh = g[rows, cols[h]]
            delta = jnp.sum(gh.astype(F32) * o.astype(F32), axis=1, keepdims=True)
            deltas.append(delta)
            total[h] = jnp.broadcast_to(delta, (BLOCK, BLOCK))
            qh = q[rows, cols[h]]
            w = nearp[h]
            gw = nt(gh, v[wide, cols[h]])
            gwg = nt(gh, vg[h])
            gs = (w[:, :band].astype(F32) * (gw - delta)).astype(BF16)
            gsg = (w[:, band:].astype(F32) * (gwg - delta)).astype(BF16)
            acc[h] = nn(gs, k[wide, cols[h]]) + nn(gsg, kg[h])
            dk_ref[wide, cols[h]] += tn(gs, qh)
            dv_ref[wide, cols[h]] += tn(w[:, :band], gh)
            dk0_ref[h] += tn(gsg, qh)
            dv0_ref[h] += tn(w[:, band:], gh)

        def backward(t, c):
            n = order[t]
            for h in range(heads):
                gw = nt(g[rows, cols[h]], slot[n, 1, :, cols[h]])
                gs = (linkp[t - begin, h].astype(F32) * (gw - total[h])).astype(BF16)
                acc[h] += nn(gs, slot[n, 0, :, cols[h]])
            return c

        lax.fori_loop(begin, end, backward, 0)
        lane = lax.broadcasted_iota(jnp.int32, (BLOCK, BLOCK), 1)
        packed = jnp.zeros((BLOCK, BLOCK), F32)
        for h in range(heads):
            dq_ref[rows, cols[h]] = (acc[h] * SCALE).astype(BF16)
            packed = jnp.where(lane == h, lses[h], packed)
            packed = jnp.where(lane == heads + h, deltas[h], packed)
        stat_ref[i] = packed.T[: 2 * heads]
        return carry

    lax.fori_loop(0, blocks, row, 0)


def own_rows(order, off, group, q, k, v, g, edge, first, slots, first_out):
    frames, width = q.shape
    heads, blocks, count = width // HEAD_DIM, frames // BLOCK, slots.shape[0]
    pad = frames + 2 * BLOCK
    tile = (heads, BLOCK, BLOCK)
    vmem = pl.BlockSpec(memory_space=pltpu.VMEM)
    return pl.pallas_call(
        rows_kernel,
        out_shape=[
            jax.ShapeDtypeStruct((frames, width), BF16),
            jax.ShapeDtypeStruct((frames, width), BF16),
            jax.ShapeDtypeStruct((pad, width), F32),
            jax.ShapeDtypeStruct((pad, width), F32),
            jax.ShapeDtypeStruct(tile, F32),
            jax.ShapeDtypeStruct(tile, F32),
            jax.ShapeDtypeStruct((blocks, 2 * heads, BLOCK), F32),
        ],
        in_specs=[SMEM] * 3 + [ANY] * 7 + [vmem],
        out_specs=[vmem] * 7,
        scratch_shapes=[
            pltpu.VMEM((frames, width), BF16),
            pltpu.VMEM((pad, width), BF16),
            pltpu.VMEM((pad, width), BF16),
            pltpu.VMEM((frames, width), BF16),
            pltpu.VMEM(slots.shape, BF16),
            pltpu.VMEM(tile, BF16),
            pltpu.VMEM(tile, BF16),
            pltpu.VMEM((heads, BLOCK, 4 * BLOCK), F32),
            pltpu.VMEM((heads, BLOCK, 4 * BLOCK), BF16),
            pltpu.VMEM((count,) + tile, F32),
            pltpu.VMEM((count,) + tile, BF16),
            pltpu.VMEM(tile, F32),
            pltpu.VMEM(tile, F32),
            pltpu.VMEM(tile, F32),
            pltpu.SemaphoreType.DMA((11,)),
        ],
        compiler_params=pltpu.CompilerParams(vmem_limit_bytes=56 << 20),
        cost_estimate=pl.CostEstimate(
            flops=20 << 30, bytes_accessed=24 << 20, transcendentals=8 << 20
        ),
        name="own_rows",
    )(order, off, group, q, k, v, g, edge, first, slots, first_out)


def columns_kernel(
    order, off, k_in, v_in, slot_in, stat_in, dk_in, dv_in, dk_ref, dv_ref,
    k, v, slot, stat, dk, dv, sem,
):
    heads = k.shape[1] // HEAD_DIM
    blocks = k.shape[0] // BLOCK
    pairs = ((k_in, k), (v_in, v), (slot_in, slot), (stat_in, stat), (dk_in, dk), (dv_in, dv))
    copies = [pltpu.make_async_copy(s, d, sem.at[n]) for n, (s, d) in enumerate(pairs)]
    for copy in copies:
        copy.start()
    for copy in copies:
        copy.wait()
    cols = [slice(h * HEAD_DIM, (h + 1) * HEAD_DIM) for h in range(heads)]

    def column(i, carry):
        rows = pl.ds(pl.multiple_of(i * BLOCK, BLOCK), BLOCK)

        def link(t, c):
            n = order[t]
            for h in range(heads):
                qs, gs = slot[n, 0, :, cols[h]], slot[n, 1, :, cols[h]]
                s = nt(k[rows, cols[h]], qs) * SCALE
                w = jnp.exp(s - stat[n, h : h + 1]).astype(BF16)
                gw = nt(v[rows, cols[h]], gs)
                d = (w.astype(F32) * (gw - stat[n, heads + h : heads + h + 1])).astype(BF16)
                dk[rows, cols[h]] += nn(d, qs)
                dv[rows, cols[h]] += nn(w, gs)
            return c

        lax.fori_loop(off[i], off[i + 1], link, 0)
        dk_ref[rows] = (dk[rows] * SCALE).astype(BF16)
        dv_ref[rows] = dv[rows].astype(BF16)
        return carry

    lax.fori_loop(0, blocks, column, 0)


def own_columns(order, off, k, v, slots, stats, dk, dv):
    frames, width = k.shape
    vmem = pl.BlockSpec(memory_space=pltpu.VMEM)
    return pl.pallas_call(
        columns_kernel,
        out_shape=[jax.ShapeDtypeStruct((frames, width), BF16)] * 2,
        in_specs=[SMEM] * 2 + [ANY] * 6,
        out_specs=[vmem] * 2,
        scratch_shapes=[
            pltpu.VMEM((frames, width), BF16),
            pltpu.VMEM((frames, width), BF16),
            pltpu.VMEM(slots.shape, BF16),
            pltpu.VMEM(stats.shape, F32),
            pltpu.VMEM((frames, width), F32),
            pltpu.VMEM((frames, width), F32),
            pltpu.SemaphoreType.DMA((6,)),
        ],
        compiler_params=pltpu.CompilerParams(vmem_limit_bytes=56 << 20),
        cost_estimate=pl.CostEstimate(
            flops=4 << 30, bytes_accessed=18 << 20, transcendentals=2 << 20
        ),
        name="own_columns",
    )(order, off, k, v, slots, stats, dk, dv)


def link_tables(rows, own, shards, per_dev):
    linked = rows.reshape(per_dev, shards, per_dev)
    block = jnp.arange(per_dev, dtype=jnp.int32)[:, None, None]
    peer = jnp.arange(shards, dtype=jnp.int32)[None, :, None]
    peer_block = jnp.arange(per_dev, dtype=jnp.int32)[None, None, :]
    own_id = own * per_dev + block
    peer_id = peer * per_dev + peer_block
    live = (
        (peer != own)
        & (linked > 0)
        & (own_id > 0)
        & (peer_id > 0)
        & (jnp.abs(own_id - peer_id) > 1)
    ).astype(jnp.int32)
    count = jnp.sum(live, axis=(0, 2))
    block_of = jnp.sum(live * block, axis=(0, 2))
    key = jnp.where(count > 0, block_of, per_dev)
    slot = jnp.arange(shards, dtype=jnp.int32)
    rank = jnp.sum(
        (
            (key[None, :] < key[:, None])
            | ((key[None, :] == key[:, None]) & (slot[None, :] < slot[:, None]))
        ).astype(jnp.int32),
        axis=1,
    )
    order = jnp.sum(slot[None, :] * (rank[None, :] == slot[:, None]).astype(jnp.int32), axis=1)
    off = jnp.sum(
        (key[None, :] < jnp.arange(per_dev + 1, dtype=jnp.int32)[:, None]).astype(jnp.int32), axis=1
    )
    return block_of, order, off


def body(query_in, key_in, value_in, out_grad, pattern):
    shards = lax.axis_size("seq")
    own = lax.axis_index("seq")
    total_blocks = pattern.shape[0]
    per_dev = total_blocks // shards
    is_first = own == 0
    rows = lax.dynamic_slice_in_dim(pattern, own * per_dev, per_dev, 0)
    block_of, order, off = link_tables(rows, own, shards, per_dev)
    group = jnp.stack((own, jnp.int32(total_blocks - 1)))

    query, key, value, grad = heads_in((query_in, key_in, value_in, out_grad), 1)
    frames, width = query.shape
    heads = width // HEAD_DIM
    edge, first = edges(query, key, value, grad, 2)
    first = first.reshape(4, heads, BLOCK, HEAD_DIM)
    q0, k0, v0, g0 = first[0], first[1], first[2], first[3]

    by_head = (frames, heads, HEAD_DIM)
    key_h, value_h = key.reshape(by_head), value.reshape(by_head)
    s0 = jnp.einsum("hqe,khe->hqk", q0, key_h, preferred_element_type=F32) * SCALE
    top0 = jnp.max(s0, axis=2)
    sum0 = jnp.sum(jnp.exp(s0 - top0[:, :, None]), axis=2)
    (parts,) = exchange(3, to_all=(jnp.concatenate((top0, sum0)),))
    tops = jnp.max(parts[:, :heads], axis=0)
    sums = jnp.sum(parts[:, heads:] * jnp.exp(parts[:, :heads] - tops[None]), axis=0)
    lse0 = tops + jnp.log(sums)
    w0 = jnp.exp(s0 - lse0[:, :, None]).astype(BF16)
    acc0 = jnp.einsum("hqk,khe->hqe", w0, value_h, preferred_element_type=F32)
    (acc_parts,) = exchange(4, to_each=(acc0.reshape(shards, 16, HEAD_DIM),))
    own_out = jnp.sum(acc_parts, axis=0).astype(BF16).astype(F32)
    (out_parts,) = exchange(5, to_all=(own_out,))
    out0 = out_parts.reshape(heads, BLOCK, HEAD_DIM)
    delta0 = jnp.sum(g0.astype(F32) * out0, axis=2)
    gw0 = jnp.einsum("hqe,khe->hqk", g0, value_h, preferred_element_type=F32)
    gs0 = (w0.astype(F32) * (gw0 - delta0[:, :, None])).astype(BF16)
    dq0 = jnp.einsum("hqk,khe->hqe", gs0, key_h, preferred_element_type=F32)
    dk_row0 = jnp.einsum("hqk,hqe->khe", gs0, q0, preferred_element_type=F32).reshape(frames, width)
    dv_row0 = jnp.einsum("hqk,hqe->khe", w0, g0, preferred_element_type=F32).reshape(frames, width)

    slot_kv = pick(block_of, key, value)
    slot_qg = pick(block_of, query, grad)
    slot_kv, out0 = lax.optimization_barrier((slot_kv, out0))
    recv_kv = lax.all_to_all(slot_kv, "seq", split_axis=0, concat_axis=0, tiled=True)
    slot_qg, recv_kv = lax.optimization_barrier((slot_qg, recv_kv))
    recv_qg = lax.all_to_all(slot_qg, "seq", split_axis=0, concat_axis=0, tiled=True)
    attended, dq, dk, dv, dk0, dv0, stats = own_rows(
        order, off, group, query, key, value, grad, edge, first, recv_kv, out0
    )
    slot_stats = jnp.take(stats, block_of, axis=0)
    unit = (shards, 16, HEAD_DIM)
    first_parts = jnp.stack((dq0.reshape(unit), dk0.reshape(unit), dv0.reshape(unit)), axis=1)
    low, high = slice(0, BLOCK), slice(BLOCK + frames, 2 * BLOCK + frames)
    sides = jnp.stack((jnp.stack((dk[high], dv[high])), jnp.stack((dk[low], dv[low]))))
    stats_in, first_sums, from_sides = exchange(
        6, to_each=(slot_stats, first_parts), to_sides=(sides,)
    )
    (totals,) = exchange(7, to_all=(jnp.sum(first_sums, axis=0),))
    totals = jnp.transpose(totals.reshape(heads, 8, 3, 16, HEAD_DIM), (2, 1, 3, 0, 4))
    totals = totals.reshape(3, BLOCK, width)
    totals = jnp.where(is_first, totals, 0.0)
    from_left = jnp.where(is_first, 0.0, from_sides[0])
    from_right = jnp.where(own == shards - 1, 0.0, from_sides[1])
    dk = dk[BLOCK : BLOCK + frames] + dk_row0
    dk = dk.at[:BLOCK].add(from_left[0] + totals[1]).at[frames - BLOCK :].add(from_right[0])
    dv = dv[BLOCK : BLOCK + frames] + dv_row0
    dv = dv.at[:BLOCK].add(from_left[1] + totals[2]).at[frames - BLOCK :].add(from_right[1])
    dq = dq.at[:BLOCK].set(jnp.where(is_first, (totals[0] * SCALE).astype(BF16), dq[:BLOCK]))
    attended_out, dq_out = heads_out((attended, dq), 8)
    dk, dv, attended_out, dq_out, recv_qg = lax.optimization_barrier(
        (dk, dv, attended_out, dq_out, recv_qg)
    )
    dk, dv = own_columns(order, off, key, value, recv_qg, stats_in, dk, dv)
    dk_out, dv_out = heads_out((dk, dv), 9)
    return attended_out, dq_out, dk_out, dv_out


def solution(mesh):
    split = P(("seq", "head"), None)
    return jax.shard_map(
        body,
        mesh=mesh,
        in_specs=(split, split, split, split, P()),
        out_specs=(split, split, split, split),
        check_vma=False,
    )
```

time: 1120 us -> 486 us (0.43); the launches traced: 1100 us -> 485 us
  Pallas kernels: 0 us -> 321 us
  waiting for transfers between devices: 363 us -> 96.2 us
  blocking collectives: 238 us -> 0 us
  local copies, waits for them, and re-layouts: 209 us -> 19.1 us
  matrix products: 102 us -> 5.98 us
  starting transfers between devices: 96.9 us -> 16.7 us
  other arithmetic: 80.2 us -> 25.4 us
  between operations: 15.2 us -> 1.11 us
    pallas_call x0 -> x13, Pallas kernels: none -> 321 us  [the longest x5 85.1 us: exchange(): pl.pallas_call(functools.partial(exchange_kernel, count, len(to_each), le...]
    psum x2 -> x0, blocking collectives: 183 us -> none  [the longest x1 126 us: body(): global_out = lax.psum(global_acc, 'seq').astype(jnp.bfloat16)]
    psum x2 -> x0, waiting for transfers between devices: 178 us -> none  [the longest x1 89.1 us: body(): lax.psum((global_dq_part, near_dk[-block_rows:], near_dv[-block_rows:]),...]
    dot_general x23 -> x6, matrix products: 102 us -> 5.98 us  [the longest x1 2.37 us: body(): acc0 = jnp.einsum('hqk,khe->hqe', w0, value_h, preferred_element_type=F32)]
    all_to_all x12 -> x2, waiting for transfers between devices: 165 us -> 96.2 us  [the longest x1 96.2 us: body(): lax.all_to_all(slot_kv, 'seq', split_axis=0, concat_axis=0, tiled=True)]
    all_to_all x12 -> x2, starting transfers between devices: 82.3 us -> 16.7 us  [the longest x1 9.77 us: body(): lax.all_to_all(slot_qg, 'seq', split_axis=0, concat_axis=0, tiled=True)]
    pmax x1 -> x0, blocking collectives: 54.8 us -> none  [body(): global_top = lax.pmax(local_top, 'seq')]
    all_to_all x14 -> x0, local copies, waits for them, and re-layouts: 38 us -> none  [the longest x1 10.4 us: body(): lax.all_to_all(part_dv, 'seq', split_axis=0, concat_axis=0, tiled=True)]
  transfers between devices with their start and end apart: 18 -> 2, of which waited for: 11 -> 1; matrix products, arithmetic and copies ran while one was open for 29% -> 6% of each run, Pallas kernels for 0% -> 31%
where the time goes in v1:
time: 486 us; the launch traced here: 485 us
  Pallas kernels  321 us (66%)
  waiting for transfers between devices  96.2 us (20%)
  other arithmetic  25.4 us (5%)
  local copies, waits for them, and re-layouts  19.1 us (4%)
  starting transfers between devices  16.7 us (3%)
  matrix products  5.98 us (1%)
    all_to_all x1, waiting for transfers between devices, body(): lax.all_to_all(slot_kv, 'seq', split_axis=0, concat_axis=0, tiled=True)  96.2 us
    pallas_call x5, Pallas kernels, exchange(): pl.pallas_call(functools.partial(exchange_kernel, count, len(to_each), le...  85.1 us
    pallas_call x1, Pallas kernels, own_rows(): pl.pallas_call(rows_kernel, out_shape=[jax.ShapeDtypeStruct((frames, widt...  63.8 us
    pallas_call x2, Pallas kernels, heads_out(): pl.pallas_call(functools.partial(heads_out_kernel, count, narr), out_shap...  51.6 us
    pallas_call x1, Pallas kernels, heads_in(): pl.pallas_call(functools.partial(heads_in_kernel, count, narr), out_shape...  50.7 us
    pallas_call x1, Pallas kernels, own_columns(): pl.pallas_call(columns_kernel, out_shape=[jax.ShapeDtypeStruct((frames, w...  32.9 us
    pallas_call x1, Pallas kernels, edges(): pl.pallas_call(functools.partial(edges_kernel, count), out_shape=[jax.Sha...  27 us
    all_to_all x1, starting transfers between devices, body(): lax.all_to_all(slot_qg, 'seq', split_axis=0, concat_axis=0, tiled=True)  9.77 us
  transfers between devices with their start and end apart: 2, of which 1 were waited for; matrix products, arithmetic and copies ran while one was open for 6% of the time, Pallas kernels for 31%

profile of v1, /device:TPU:32, one launch (start us, length us, event | category | flops | bytes accessed | tf_op | source)
XLA Modules:
  0.0 485.1 jit_solution(4077664124741972676)
XLA Ops:
  0.7 50.7 %heads_in.1 = (bf16[4,256,512]{2,1,0:T(8,128)(2,1)}, bf16[4,256,512]{2,1,0:T(8,128)(2,1)}, bf16[4,256,512]{2,1,0:T(8,128)(2,1)}, bf16[4,256,512]{2,1,0:T(8,128)(2,1)}) custom-call(bf16[256,2048]{1,0:T(8,128)(2,1)} %refs_0_.1, bf16[256,2048]{1,0:T(8,128)(2,1)} %refs_1_.1, bf16[256,2048]{1,0:T(8,128)(2,1)} %refs_2_.1, bf16[256,2048]{1,0:T(8,128)(2,1)} %refs_3_.1), custom_call_target="tpu_custom_call" | custom-call | tf_op jit(solution)/shard_map/heads_in/pallas_call | solution.py:81
  51.4 2.2 reshape_reshape.6
  53.7 1.1 reshape_reshape.7
  54.7 27.0 %edges.1 = (bf16[2,2,128,512]{3,2,1,0:T(8,128)(2,1)}, bf16[4,32,16,128]{3,2,1,0:T(8,128)(2,1)}) custom-call(bf16[1024,512]{1,0:T(8,128)(2,1)} %bitcast.112, bf16[1024,512]{1,0:T(8,128)(2,1)} %bitcast.102, bf16[1024,512]{1,0:T(8,128)(2,1)} %bitcast.106, bf16[1024,512]{1,0:T(8,128)(2,1)} %bitcast.115), custom_call_target="tpu_custom_call" | custom-call | tf_op jit(solution)/shard_map/edges/pallas_call | solution.py:249
  84.3 10.3 %exchange.5 = f32[32,8,128]{2,1,0:T(8,128)} custom-call(f32[8,128]{1,0:T(8,128)} %pad_maximum_fusion.2.refs_0_), custom_call_target="tpu_custom_call" | custom-call | tf_op jit(solution)/shard_map/exchange/pallas_call | solution.py:337
  97.0 2.4 fusion.1
  99.4 10.3 %exchange.6 = f32[32,16,128]{2,1,0:T(8,128)} custom-call(f32[32,16,128]{2,1,0:T(8,128)} %bitcast.127), custom_call_target="tpu_custom_call" | custom-call | tf_op jit(solution)/shard_map/exchange/pallas_call | solution.py:337
  111.4 10.2 %exchange.7 = f32[32,16,128]{2,1,0:T(8,128)} custom-call(f32[16,128]{1,0:T(8,128)} %convert_element_type.62.refs_0_), custom_call_target="tpu_custom_call" | custom-call | tf_op jit(solution)/shard_map/exchange/pallas_call | solution.py:337
  123.5 4.8 pick.3
  128.3 7.0 %all-to-all-start = ((bf16[32,2,128,512]{3,2,1,0:T(8,128)(2,1)}), bf16[32,2,128,512]{3,2,1,0:T(8,128)(2,1)}, u32[]{:S(2)}, u32[]{:S(2)}) async-start(bf16[32,2,128,512]{3,2,1,0:T(8,128)(2,1)} %pick.3), calls=%async_computation | async-start | bytes 16777216 | tf_op jit(solution)/shard_map/all_to_all | solution.py:693
  135.3 4.8 pick.2
  140.1 96.2 %all-to-all-done.slot_in = bf16[32,2,128,512]{3,2,1,0:T(8,128)(2,1)} async-done(((bf16[32,2,128,512]{3,2,1,0:T(8,128)(2,1)}), bf16[32,2,128,512]{3,2,1,0:T(8,128)(2,1)}, u32[]{:S(2)}, u32[]{:S(2)}) %all-to-all-start) | async-done | bytes 8388640 | tf_op jit(solution)/shard_map/all_to_all | solution.py:693
  236.3 9.8 %all-to-all-start.1 = ((bf16[32,2,128,512]{3,2,1,0:T(8,128)(2,1)}), bf16[32,2,128,512]{3,2,1,0:T(8,128)(2,1)}, u32[]{:S(2)}, u32[]{:S(2)}) async-start(bf16[32,2,128,512]{3,2,1,0:T(8,128)(2,1)} %pick.2), calls=%async_computation.1 | async-start | bytes 16777216 | tf_op jit(solution)/shard_map/all_to_all | solution.py:695
  246.3 1.0 fusion.20
  249.3 1.8 copy.38
  251.7 1.8 copy.39
  255.6 1.7 fusion.3
  257.2 63.8 %own_rows.1 = (bf16[1024,512]{1,0:T(8,128)(2,1)}, bf16[1024,512]{1,0:T(8,128)(2,1)}, f32[1280,512]{1,0:T(8,128)}, f32[1280,512]{1,0:T(8,128)}, f32[4,128,128]{2,...) custom-call(s32[32]{0:T(128)} %select_reduce_fusion.order, s32[9]{0:T(128)} %convert_reduce_fusion.1.off, ...), custom_call_target="tpu_custom_call" | custom-call | flops 21474836480 | bytes 25165824 | tf_op jit(solution)/shard_map/own_rows/pallas_call | solution.py:519
  321.0 1.3 gather_fusion
  322.4 1.3 slice_bitcast_fusion.6
  324.8 1.0 pad_maximum_fusion.refs_2_
  326.6 34.6 %exchange.8 = (f32[32,8,128]{2,1,0:T(8,128)}, f32[32,3,16,128]{3,2,1,0:T(8,128)}, f32[2,2,128,512]{3,2,1,0:T(8,128)}) custom-call(f32[32,8,128]{2,1,0:T(8,128)} %broadcast_select_fusion.1.refs_0_, f32[32,3,16,128]{3,2,1,0:T(8,128)} %pad_maximum_fusion.1.refs_1_, f32[2,2,128,512]{3,2,1,0:T(8,128)} %pad_maximum_fusion.refs_2_), custom_call_target="tpu_custom_call" | custom-call | tf_op jit(solution)/shard_map/exchange/pallas_call | solution.py:337
  361.2 1.8 reduce_sum.120.refs_0_
  363.0 19.7 %exchange.9 = f32[32,3,16,128]{3,2,1,0:T(8,128)} custom-call(f32[3,16,128]{2,1,0:T(8,128)} %reduce_sum.120.refs_0_), custom_call_target="tpu_custom_call" | custom-call | tf_op jit(solution)/shard_map/exchange/pallas_call | solution.py:337
  384.3 1.6 fusion.21.refs_1_
  385.9 27.2 %heads_out.2 = (bf16[256,2048]{1,0:T(8,128)(2,1)}, bf16[256,2048]{1,0:T(8,128)(2,1)}) custom-call(bf16[1024,512]{1,0:T(8,128)(2,1)} %get-tuple-element.111.refs_0_, bf16[1024,512]{1,0:T(8,128)(2,1)} %fusion.21.refs_1_), custom_call_target="tpu_custom_call" | custom-call | tf_op jit(solution)/shard_map/heads_out/pallas_call | solution.py:135
  413.3 1.5 copy-done.2
  414.7 5.2 %slice_add_fusion = (f32[1024,512]{1,0:T(8,128)}, f32[1024,512]{1,0:T(8,128)}) fusion(f32[1024,512]{1,0:T(8,128)S(1)} %copy-done.2, f32[1280,512]{1,0:T(8,128)} %get-tuple-element.108, f32[1024,512]{1,0:T(8,128)S(1)} %copy-done.1, f32[1280,512]{1,0:T(8,128)} %get-tuple-element.104), kind=kLoop, calls=%fused_computation.1 | loop fusion | flops 1048576 | bytes 12582912 | tf_op jit(solution)/shard_map/add | solution.py:715
  419.9 2.0 fusion.13
  421.9 1.9 fusion.9
  423.9 32.9 %own_columns.1 = (bf16[1024,512]{1,0:T(8,128)(2,1)}, bf16[1024,512]{1,0:T(8,128)(2,1)}) custom-call(s32[32]{0:T(128)} %select_reduce_fusion.order, s32[9]{0:T(128)} %convert_reduce_fusion.1.off, bf16[1024,512]{1,0:T(8,128)(2,1)} %bitcast.105, bf16[1024,512]{1,0:T(8,128)(2,1)} %bitcast.109, bf16[32,2,128,512]{3,2,1,0:T(8,128)(2,1)} %all-to-all-done.1.slot_in, ...), custom_call_target="tpu_custom_call" | custom-call | flops 4294967296 | bytes 18874368 | tf_op jit(solution)/shard_map/own_columns/pallas_call | solution.py:597
  456.8 24.4 %heads_out.3 = (bf16[256,2048]{1,0:T(8,128)(2,1)}, bf16[256,2048]{1,0:T(8,128)(2,1)}) custom-call(bf16[1024,512]{1,0:T(8,128)(2,1)} %get-tuple-element.122.refs_0_, bf16[1024,512]{1,0:T(8,128)(2,1)} %get-tuple-element.123.refs_1_), custom_call_target="tpu_custom_call" | custom-call | tf_op jit(solution)/shard_map/heads_out/pallas_call | solution.py:135
  (86 shorter events, 20.7 us)
Async XLA Ops:
  51.4 2.2 copy-start
  54.7 28.0 %copy-start.5 = (bf16[1024,4,128]{2,1,0:T(4,128)(2,1)S(1)}, bf16[1024,4,128]{2,1,0:T(4,128)(2,1)}, u32[]{:S(2)}) copy-start(bf16[1024,4,128]{2,1,0:T(4,128)(2,1)} %reshape_reshape.6) | copy-start | bytes 3145732
  128.3 108.0 %all-to-all-start = ((bf16[32,2,128,512]{3,2,1,0:T(8,128)(2,1)}), bf16[32,2,128,512]{3,2,1,0:T(8,128)(2,1)}, u32[]{:S(2)}, u32[]{:S(2)}) async-start(bf16[32,2,128,512]{3,2,1,0:T(8,128)(2,1)} %pick.3), calls=%async_computation | async-start | bytes 16777216 | tf_op jit(solution)/shard_map/all_to_all | solution.py:693
  140.0 106.2 %copy-start.11 = (f32[32,16,128]{2,1,0:T(8,128)S(1)}, f32[32,16,128]{2,1,0:T(8,128)}, u32[]{:S(2)}) copy-start(f32[32,16,128]{2,1,0:T(8,128)} %exchange.7) | copy-start | bytes 786436
  140.1 107.3 %copy-start.6 = (bf16[1024,4,128]{2,1,0:T(4,128)(2,1)S(1)}, bf16[1024,4,128]{2,1,0:T(4,128)(2,1)}, u32[]{:S(2)}) copy-start(bf16[1024,4,128]{2,1,0:T(4,128)(2,1)} %reshape_reshape.7) | copy-start | bytes 3145732
  236.3 187.6 %all-to-all-start.1 = ((bf16[32,2,128,512]{3,2,1,0:T(8,128)(2,1)}), bf16[32,2,128,512]{3,2,1,0:T(8,128)(2,1)}, u32[]{:S(2)}, u32[]{:S(2)}) async-start(bf16[32,2,128,512]{3,2,1,0:T(8,128)(2,1)} %pick.2), calls=%async_computation.1 | async-start | bytes 16777216 | tf_op jit(solution)/shard_map/all_to_all | solution.py:695
  247.9 1.0 copy-start.3
  251.6 2.5 copy-start.16
  251.7 3.9 copy-start.4
  322.4 1.4 copy-start.14
  322.4 1.4 copy-start.15
  383.4 29.8 %copy-start.12 = (f32[2,2,128,512]{3,2,1,0:T(8,128)S(1)}, f32[2,2,128,512]{3,2,1,0:T(8,128)}, u32[]{:S(2)}) copy-start(f32[2,2,128,512]{3,2,1,0:T(8,128)} %get-tuple-element.109) | copy-start | bytes 3145732
  385.9 27.4 %copy-start.1 = (f32[1024,512]{1,0:T(8,128)S(1)}, f32[1024,512]{1,0:T(8,128)}, u32[]{:S(2)}) copy-start(f32[1024,512]{1,0:T(8,128)} %copy.38) | copy-start | bytes 6291460
  413.1 1.6 copy-start.2
  414.7 5.2 %copy-start.13 = (f32[1,128,512]{2,1,0:T(8,128)S(1)}, f32[1,128,512]{2,1,0:T(8,128)}, u32[]{:S(2)}) copy-start(f32[1,128,512]{2,1,0:T(8,128)} %slice.194) | copy-start | bytes 786436
  456.8 24.4 %copy-start.8 = (bf16[256,2048]{1,0:T(8,128)(2,1)S(1)}, bf16[256,2048]{1,0:T(8,128)(2,1)}, u32[]{:S(2)}) copy-start(bf16[256,2048]{1,0:T(8,128)(2,1)} %get-tuple-element.155) | copy-start | bytes 3145732
  456.8 25.4 %copy-start.7 = (bf16[256,2048]{1,0:T(8,128)(2,1)S(1)}, bf16[256,2048]{1,0:T(8,128)(2,1)}, u32[]{:S(2)}) copy-start(bf16[256,2048]{1,0:T(8,128)(2,1)} %get-tuple-element.156) | copy-start | bytes 3145732
  481.2 2.0 copy-start.10
  482.2 1.9 copy-start.9

commit v2 on v0

v2 whole, which is shorter than its diff:
```python
import functools

import jax
import jax.numpy as jnp
from jax import lax
from jax.experimental import pallas as pl
from jax.experimental.pallas import tpu as pltpu
from jax.sharding import PartitionSpec as P

D = 128
B = 128
HEADS = 4
BLOCKS = 8
SEQ = 32
YS = 4
SCALE = D ** (-0.5)
NEG = -1e30
MESH = pl.DeviceIdType.MESH
F32, BF16 = jnp.float32, jnp.bfloat16
KV, QG = 0, 1
GROUPS = ((KV, 0), (KV, 1), (QG, 0), (KV, 2), (QG, 1), (KV, 3), (QG, 2), (QG, 3))
ARRIVALS = ((KV, 0), (KV, 1), (QG, 0), (KV, 2), (KV, 3), (QG, 1), (QG, 2), (QG, 3))
PER_GROUP = 4
BATCHES = ((1, 8), (8, 16), (16, 24), (24, 32))
RING = 4
EARLY = 3
AHEAD = 4


def nt(a, b):
    return lax.dot_general(a, b, (((1,), (1,)), ((), ())), preferred_element_type=F32)


def tn(a, b):
    return lax.dot_general(a, b, (((0,), (0,)), ((), ())), preferred_element_type=F32)


def nn(a, b):
    return jnp.dot(a, b, preferred_element_type=F32)


def loop(count, step, init, by=4):
    def some(n, carry):
        for m in range(by):
            carry = step(n * by + m, carry)
        return carry

    return lax.fori_loop(0, count // by, some, init)


def take_all(ref, sem):
    pltpu.make_async_copy(ref, ref, sem).wait()


def kernel(
    block_of, order, key, same, tail, has, live,
    k_in, v_in, q_in, g_in, o_out, dq_out, dk_out, dv_out,
    kv, qg, edge, stage, got, stat_out, stat_got, dgrad, side, staged,
    kpad, ns, npr, ls, lp, run_a, run_b, topb, lseb, delb, oacc, stat,
    fb, first, p0, ml_out, ml_got, acc_out, acc_got, o_own, o0, dq0, dk0, dv0,
    rs_out, rs_got, t_own, t_got,
    y_send, y_recv, y_local, fb_sem, sc_sem, ag_sem, bulk_send, bulk_recv, halo_sem, side_sem,
    ml_sem, acc_sem, o_sem, stat_sem, rs_sem, t_sem, out_sem,
):
    me, ym = lax.axis_index("seq"), lax.axis_index("head")
    mz, mx, mc = me // 8, lax.rem(me // 2, 4), lax.rem(me, 2)
    right, left = lax.rem(me + 1, SEQ), lax.rem(me + SEQ - 1, SEQ)
    ins = ((k_in, v_in), (q_in, g_in))
    own = (kv, qg)
    outs = (o_out, dq_out, dk_out, dv_out)
    is_root = me == 0

    def to_seq(src, dst, send, recv, peer):
        return pltpu.make_async_remote_copy(
            src_ref=src, dst_ref=dst, send_sem=send, recv_sem=recv,
            device_id={"seq": peer}, device_id_type=MESH,
        )

    def to_head(src, dst, send, recv, peer):
        return pltpu.make_async_remote_copy(
            src_ref=src, dst_ref=dst, send_sem=send, recv_sem=recv,
            device_id={"head": peer}, device_id_type=MESH,
        )

    def to_all(copy_to):
        def start(step, c):
            copy_to(lax.rem(me + step, SEQ)).start()
            return c

        lax.fori_loop(1, SEQ, start, 0)

    sem = pltpu.get_barrier_semaphore()

    def greet(step, c):
        pl.semaphore_signal(
            sem, inc=1, device_id={"seq": lax.rem(me + step, SEQ)}, device_id_type=MESH
        )
        return c

    lax.fori_loop(1, SEQ, greet, 0)
    for step in range(1, YS):
        pl.semaphore_signal(
            sem, inc=1, device_id={"head": lax.rem(ym + step, YS)}, device_id_type=MESH
        )
    pl.semaphore_wait(sem, SEQ - 1 + YS - 1)

    def columns(y, h):
        return pl.ds(pl.multiple_of((y * HEADS + h) * D, D), D)

    @pl.when(is_root & (ym == 0))
    def _():
        for p in range(2):
            for a in range(2):

                def give(n, c, p=p, a=a):
                    to_head(
                        ins[p][a].at[0, :, pl.ds(pl.multiple_of(n * D, D), D)],
                        fb.at[2 * p + a, lax.rem(n, HEADS)],
                        fb_sem.at[0], fb_sem.at[1], n // HEADS,
                    ).start()
                    return c

                lax.fori_loop(HEADS, YS * HEADS, give, 0)

                def hold(h, c, p=p, a=a):
                    pltpu.make_async_copy(
                        ins[p][a].at[0, :, pl.ds(pl.multiple_of(h * D, D), D)],
                        fb.at[2 * p + a, h],
                        fb_sem.at[2],
                    ).start()
                    return c

                lax.fori_loop(0, HEADS, hold, 0)

    def enter(p, h):
        for a in range(2):

            def give(step, c, a=a):
                peer = lax.rem(ym + step, YS)
                to_head(
                    ins[p][a].at[:, :, columns(peer, h)],
                    own[p][h].at[a, pl.ds(2 * ym, 2)],
                    y_send.at[p, h], y_recv.at[p, h], peer,
                ).start()
                return c

            lax.fori_loop(1, YS, give, 0)
            pltpu.make_async_copy(
                ins[p][a].at[:, :, columns(ym, h)],
                own[p][h].at[a, pl.ds(2 * ym, 2)],
                y_local.at[p, h],
            ).start()

    entering = list(ARRIVALS)

    def enter_next():
        if entering:
            enter(*entering.pop(0))

    for _ in range(EARLY):
        enter_next()
    for h in range(HEADS):
        for p in range(2):
            for n in range(BLOCKS + 2):
                dgrad[h][p, n] = jnp.zeros((B, D), F32)
    dk0[...] = jnp.zeros_like(dk0)
    dv0[...] = jnp.zeros_like(dv0)

    arrived = set()

    def arrive(p, h):
        if (p, h) in arrived:
            return
        arrived.add((p, h))
        enter_next()
        take_all(own[p][h].at[:, pl.ds(0, 6)], y_recv.at[p, h])
        take_all(own[p][h].at[:, pl.ds(0, 2)], y_local.at[p, h])
        if p == KV:
            to_seq(
                kv[h].at[:, BLOCKS - 1], edge[h].at[0], halo_sem.at[0, h], halo_sem.at[1, h], right
            ).start()
            to_seq(
                kv[h].at[:, 0], edge[h].at[1], halo_sem.at[2, h], halo_sem.at[3, h], left
            ).start()

    state = {"next": 0, "picked": 0}

    def sent(batch):
        begin, end = BATCHES[batch % PER_GROUP]
        buffer = stage[(batch // PER_GROUP) % RING]
        take_all(buffer.at[pl.ds(0, end - begin)], bulk_send.at[batch])

    def choose(n):
        p, h = GROUPS[n]
        arrive(p, h)
        buffer = stage[n % RING]

        def one(s, c):
            buffer[s, 0] = own[p][h][0, block_of[s]]
            buffer[s, 1] = own[p][h][1, block_of[s]]
            return c

        lax.fori_loop(0, SEQ, one, 0)

    def pump(upto=None):
        batch = state["next"]
        if batch >= PER_GROUP * len(GROUPS):
            return
        if upto is not None:
            while state["next"] < min(upto, PER_GROUP * len(GROUPS)):
                pump()
            return
        state["next"] += 1
        if batch >= AHEAD:
            sent(batch - AHEAD)
        n = batch // PER_GROUP
        if batch % PER_GROUP == 0:
            choose(n)
        p, h = GROUPS[n]

        def start(step, c):
            z = lax.rem(step, 4)
            x = lax.rem(step // 4 + z, 4)
            peer = lax.rem(mz + z, 4) * 8 + lax.rem(mx + x, 4) * 2 + lax.rem(mc + step // 16, 2)
            to_seq(
                stage[n % RING].at[peer], got[p][h].at[me],
                bulk_send.at[batch], bulk_recv.at[p, h], peer,
            ).start()
            return c

        lax.fori_loop(*BATCHES[batch % PER_GROUP], start, 0)

    posted = {}

    def post(name):
        posted[name] = state["next"]

    def due(name):
        pump(posted[name] + AHEAD)

    landed = set()

    def linked(p, h):
        if (p, h) in landed:
            return
        landed.add((p, h))
        n = GROUPS.index((p, h))
        pump(PER_GROUP * (n + 1) + AHEAD - 1)
        take_all(got[p][h].at[pl.ds(0, SEQ - 1)], bulk_recv.at[p, h])

    def piece(ref, unit):
        rows = pl.ds(pl.multiple_of(lax.rem(unit, 8) * 16, 16), 16)
        return ref.at[:, unit // 8, rows]

    @pl.when(is_root)
    def _():
        @pl.when(ym == 0)
        def _():
            take_all(fb, fb_sem.at[2])

        @pl.when(ym > 0)
        def _():
            take_all(fb, fb_sem.at[1])

        to_all(
            lambda peer: to_seq(piece(fb, peer), piece(first, peer), sc_sem.at[0], sc_sem.at[1], peer)
        )
        first[:, 0, pl.ds(0, 16)] = fb[:, 0, pl.ds(0, 16)]

    @pl.when(me > 0)
    def _():
        take_all(piece(first, me), sc_sem.at[1])

    to_all(lambda peer: to_seq(piece(first, me), piece(first, me), ag_sem.at[0], ag_sem.at[1], peer))
    arrive(KV, 0)
    pump(PER_GROUP)

    @pl.when(is_root & (ym == 0))
    def _():
        take_all(stage[1].at[pl.ds(0, 24)], fb_sem.at[0])

    arrive(KV, 1)
    pump()
    arrive(QG, 0)
    arrive(KV, 2)
    pump()
    arrive(KV, 3)
    pieces = lp.at[pl.ds(0, SEQ - 1), pl.ds(0, B // 2)]
    take_all(pieces, ag_sem.at[1])

    lanes = lax.broadcasted_iota(jnp.int32, (B, B), 1)

    def scores0(h, n):
        return nt(first[2, h], kv[h][0, n]) * SCALE

    packed = jnp.zeros((B, B), F32)
    for h in range(HEADS):
        tops = loop(BLOCKS, lambda n, c, h=h: jnp.maximum(c, scores0(h, n)), jnp.full((B, B), NEG, F32))
        m0 = jnp.max(tops, axis=1, keepdims=True)
        l0 = loop(BLOCKS, lambda n, c, h=h, m0=m0: c + jnp.exp(scores0(h, n) - m0), jnp.zeros((B, B), F32))
        packed = jnp.where(lanes == h, m0, packed)
        packed = jnp.where(lanes == HEADS + h, jnp.sum(l0, axis=1, keepdims=True), packed)
    ml_out[...] = packed.T[: 2 * HEADS]
    to_all(lambda peer: to_seq(ml_out, ml_got.at[me], ml_sem.at[0], ml_sem.at[1], peer))
    ml_got[me] = ml_out[...]
    post("ml")

    def rows_one(h):
        linked(KV, h)
        take_all(edge[h].at[0], halo_sem.at[1, h])
        take_all(edge[h].at[1], halo_sem.at[3, h])
        slot = got[KV][h]
        arrive(QG, h)
        for a in range(2):
            kpad[a, 0] = edge[h][0, a]
            kpad[a, pl.ds(1, BLOCKS)] = kv[h][a]
            kpad[a, BLOCKS + 1] = edge[h][1, a]

        def score(t, c):
            s = nt(qg[h][0, key[t]], slot[order[t], 0]) * SCALE
            s = s + jnp.where(t < live[0], 0.0, NEG)
            ls[t] = s
            run_a[t + 1] = jnp.maximum(s, run_a[t] + jnp.where(same[t] > 0, 0.0, NEG))
            return c

        run_a[0] = jnp.zeros((B, B), F32)
        loop(SEQ, score, 0)
        pump()

        def near_score(i, c):
            q = qg[h][0, i]
            band = kpad[0, pl.ds(i, 3)].reshape(3 * B, D)
            ids = me * BLOCKS + i - 1 + lax.broadcasted_iota(jnp.int32, (1, 3 * B), 1) // B
            s = nt(q, band) * SCALE + jnp.where((ids > 0) & (ids < SEQ * BLOCKS), 0.0, NEG)
            sg = nt(q, first[0, h]) * SCALE
            ns[i, :, pl.ds(0, 3 * B)] = s
            ns[i, :, pl.ds(3 * B, B)] = sg
            top = jnp.maximum(
                jnp.maximum(s[:, :B], s[:, B : 2 * B]), jnp.maximum(s[:, 2 * B :], sg)
            )
            top = jnp.maximum(top, jnp.where(has[i] > 0, run_a[tail[i]], NEG))
            topb[i] = jnp.broadcast_to(jnp.max(top, axis=1, keepdims=True), (B, B))
            return c

        loop(BLOCKS, near_score, 0, by=2)

        def expo(t, c):
            e = jnp.exp(ls[t] - topb[key[t]])
            run_a[t + 1] = e + run_a[t] * same[t].astype(F32)
            return c

        loop(SEQ, expo, 0)
        pump()

        def near_weights(i, c):
            m = topb[i][:, :1]
            e = jnp.exp(ns[i] - m)
            e = (e[:, :B] + e[:, B : 2 * B]) + (e[:, 2 * B : 3 * B] + e[:, 3 * B :])
            e = e + jnp.where(has[i] > 0, run_a[tail[i]], 0.0)
            lse = m + jnp.log(jnp.sum(e, axis=1, keepdims=True))
            lseb[i] = jnp.broadcast_to(lse, (B, B))
            keep = jnp.where(me * BLOCKS + i > 0, 1.0, 0.0)
            w = (jnp.exp(ns[i] - lse) * keep).astype(BF16)
            npr[i] = w
            oacc[i] = nn(w[:, : 3 * B], kpad[1, pl.ds(i, 3)].reshape(3 * B, D)) + nn(
                w[:, 3 * B :], first[1, h]
            )
            return c

        loop(BLOCKS, near_weights, 0, by=2)

        def attend(t, c):
            w = jnp.exp(ls[t] - lseb[key[t]]).astype(BF16)
            lp[t] = w
            run_a[t + 1] = nn(w, slot[order[t], 1]) + run_a[t] * same[t].astype(F32)
            return c

        loop(SEQ, attend, 0)
        pump()

        def near_back(i, c):
            o = (oacc[i] + jnp.where(has[i] > 0, run_a[tail[i]], 0.0)).astype(BF16)
            staged[0][h][i] = o
            g, q = qg[h][1, i], qg[h][0, i]
            delta = jnp.sum(g.astype(F32) * o.astype(F32), axis=1, keepdims=True)
            delb[i] = jnp.broadcast_to(delta, (B, B))
            both = jnp.where(lanes == 0, lseb[i], delb[i])
            stat[i] = both.T[:8]
            w = npr[i]
            gw = nt(g, kpad[1, pl.ds(i, 3)].reshape(3 * B, D))
            gwg = nt(g, first[1, h])
            gs = (w[:, : 3 * B].astype(F32) * (gw - delta)).astype(BF16)
            gsg = (w[:, 3 * B :].astype(F32) * (gwg - delta)).astype(BF16)
            oacc[i] = nn(gs, kpad[0, pl.ds(i, 3)].reshape(3 * B, D)) + nn(gsg, first[0, h])
            dgrad[h][0, pl.ds(i, 3)] += tn(gs, q).reshape(3, B, D)
            dgrad[h][1, pl.ds(i, 3)] += tn(w[:, : 3 * B], g).reshape(3, B, D)
            dk0[h] += tn(gsg, q)
            dv0[h] += tn(w[:, 3 * B :], g)
            return c

        loop(BLOCKS, near_back, 0, by=2)

        def stat_of(s, c):
            stat_out[h][s] = stat[block_of[s]]
            return c

        lax.fori_loop(0, SEQ, stat_of, 0)
        to_all(
            lambda peer: to_seq(
                stat_out[h].at[peer], stat_got[h].at[me], stat_sem.at[0, h], stat_sem.at[1, h], peer
            )
        )
        stat_got[h][me] = stat_out[h][me]
        post(("stat", h))
        to_seq(
            dgrad[h].at[:, BLOCKS + 1], side[h].at[0], side_sem.at[0, h], side_sem.at[1, h], right
        ).start()
        to_seq(dgrad[h].at[:, 0], side[h].at[1], side_sem.at[2, h], side_sem.at[3, h], left).start()
        pump()

        def back(t, c):
            gw = nt(qg[h][1, key[t]], slot[order[t], 1])
            gs = (lp[t].astype(F32) * (gw - delb[key[t]])).astype(BF16)
            run_a[t + 1] = nn(gs, slot[order[t], 0]) + run_a[t] * same[t].astype(F32)
            return c

        loop(SEQ, back, 0)

        def query_grad(i, c):
            dq = oacc[i] + jnp.where(has[i] > 0, run_a[tail[i]], 0.0)
            staged[1][h][i] = (dq * SCALE).astype(BF16)
            return c

        loop(BLOCKS, query_grad, 0)

    def leave(a, h, step, block):
        peer = lax.rem(ym + step, YS)
        return to_head(
            staged[a][h].at[pl.ds(2 * peer + block, 1)],
            outs[a].at[pl.ds(block, 1), :, columns(ym, h)],
            out_sem.at[0, a], out_sem.at[1, a], peer,
        )

    def remain(a, h, block):
        return pltpu.make_async_copy(
            staged[a][h].at[pl.ds(2 * ym + block, 1)],
            outs[a].at[pl.ds(block, 1), :, columns(ym, h)],
            out_sem.at[2, a],
        )

    def depart(a, h):
        remain(a, h, 1).start()

        def ahead(step, c):
            leave(a, h, step, 1).start()
            return c

        lax.fori_loop(1, YS, ahead, 0)

        @pl.when(jnp.logical_not(is_root & (ym == 0)) | (a == 0))
        def _():
            remain(a, h, 0).start()

        def rest(step, c):
            @pl.when(jnp.logical_not(is_root & (lax.rem(ym + step, YS) == 0)) | (a == 0))
            def _():
                leave(a, h, step, 0).start()

            return c

        lax.fori_loop(1, YS, rest, 0)

    def columns_one(h):
        linked(QG, h)
        due(("stat", h))
        take_all(stat_got[h].at[pl.ds(0, SEQ - 1)], stat_sem.at[1, h])
        slot, stats = got[QG][h], stat_got[h]

        def link(t, c):
            n, b = order[t], key[t]
            q, g = slot[n, 0], slot[n, 1]
            st = stats[n]
            s = nt(kv[h][0, b], q) * SCALE
            w = jnp.exp(s - st[0:1]).astype(BF16)
            gw = nt(kv[h][1, b], g)
            d = (w.astype(F32) * (gw - st[1:2])).astype(BF16)
            f = same[t].astype(F32)
            run_a[t + 1] = nn(d, q) + run_a[t] * f
            run_b[t + 1] = nn(w, g) + run_b[t] * f
            return c

        run_a[0] = jnp.zeros((B, D), F32)
        run_b[0] = jnp.zeros((B, D), F32)
        loop(SEQ, link, 0)
        pump()
        take_all(side[h].at[0], side_sem.at[1, h])
        take_all(side[h].at[1], side_sem.at[3, h])
        not_first = jnp.where(me > 0, 1.0, 0.0)
        not_last = jnp.where(me < SEQ - 1, 1.0, 0.0)

        def final(i, c):
            at_low = jnp.where(i == 0, not_first, 0.0)
            at_high = jnp.where(i == BLOCKS - 1, not_last, 0.0)
            for a, run in enumerate((run_a, run_b)):
                d = dgrad[h][a, i + 1] + jnp.where(has[i] > 0, run[tail[i]], 0.0)
                d = d + side[h][0, a] * at_low + side[h][1, a] * at_high
                dgrad[h][a, i + 1] = d
                staged[2 + a][h][i] = (d * (SCALE if a == 0 else 1.0)).astype(BF16)
            return c

        loop(BLOCKS, final, 0, by=2)
        depart(2, h)
        depart(3, h)

    rows_one(0)

    due("ml")
    take_all(ml_got.at[pl.ds(0, SEQ - 1)], ml_sem.at[1])
    parts = ml_got[...]
    tops = jnp.max(parts[:, :HEADS], axis=0)
    sums = jnp.sum(parts[:, HEADS:] * jnp.exp(parts[:, :HEADS] - tops[None]), axis=0)
    lse_rows = jnp.concatenate((tops + jnp.log(sums), jnp.zeros((B - HEADS, B), F32)))
    lse_cols = lse_rows.T
    for h in range(HEADS):
        lse = lse_cols[:, h : h + 1]

        def weigh(n, c, h=h, lse=lse):
            w = jnp.exp(scores0(h, n) - lse).astype(BF16)
            p0[h, n] = w
            return c + nn(w, kv[h][1, n])

        a0 = loop(BLOCKS, weigh, jnp.zeros((B, D), F32))
        acc_out[pl.ds(h * 8, 8)] = a0.reshape(8, 16, D)
    to_all(
        lambda peer: to_seq(acc_out.at[peer], acc_got.at[me], acc_sem.at[0], acc_sem.at[1], peer)
    )
    acc_got[me] = acc_out[me]
    post("acc")

    rows_one(1)

    due("acc")
    take_all(acc_got.at[pl.ds(0, SEQ - 1)], acc_sem.at[1])
    o_own[...] = jnp.sum(acc_got[...], axis=0).astype(BF16).astype(F32)
    to_all(lambda peer: to_seq(o_own, o0.at[me], o_sem.at[0], o_sem.at[1], peer))
    o0[me] = o_own[...]
    post("o")
    linked(QG, 0)
    due("o")
    take_all(o0.at[pl.ds(0, SEQ - 1)], o_sem.at[1])

    for h in range(HEADS):
        g, q = first[3, h], first[2, h]
        o = o0[pl.ds(h * 8, 8)].reshape(B, D)
        delta = jnp.sum(g.astype(F32) * o, axis=1, keepdims=True)

        def back0(n, c, h=h, g=g, q=q, delta=delta):
            w = p0[h, n]
            gs = (w.astype(F32) * (nt(g, kv[h][1, n]) - delta)).astype(BF16)
            dgrad[h][0, n + 1] += tn(gs, q)
            dgrad[h][1, n + 1] += tn(w, g)
            return c + nn(gs, kv[h][0, n])

        dq0[h] = loop(BLOCKS, back0, jnp.zeros((B, D), F32), by=2)

    def departs(h):
        @pl.when(is_root)
        def _():
            staged[0][h][0] = o0[pl.ds(h * 8, 8)].reshape(B, D).astype(BF16)

        depart(0, h)
        depart(1, h)

    departs(0)
    departs(1)
    pump()

    columns_one(0)
    rows_one(2)
    departs(2)
    columns_one(1)
    rows_one(3)
    departs(3)

    for h in range(HEADS):
        for n, ref in enumerate((dq0, dk0, dv0)):
            rs_out[pl.ds(h * 8, 8), n] = ref[h].reshape(8, 16, D)
    to_all(lambda peer: to_seq(rs_out.at[peer], rs_got.at[me], rs_sem.at[0], rs_sem.at[1], peer))
    rs_got[me] = rs_out[me]
    columns_one(2)
    pump(PER_GROUP * len(GROUPS))
    take_all(rs_got.at[pl.ds(0, SEQ - 1)], rs_sem.at[1])
    t_own[...] = jnp.sum(rs_got[...], axis=0)

    @pl.when(me > 0)
    def _():
        to_seq(t_own, t_got.at[me], t_sem.at[0], t_sem.at[1], 0).start()

    columns_one(3)

    @pl.when(is_root)
    def _():
        t_got[0] = t_own[...]
        take_all(t_got.at[pl.ds(0, SEQ - 1)], t_sem.at[1])
        for h in range(HEADS):
            dq, dk, dv = (t_got[pl.ds(h * 8, 8), n].reshape(B, D) for n in range(3))
            staged[1][h][0] = (dq * SCALE).astype(BF16)
            staged[2][h][0] = ((dgrad[h][0, 1] + dk) * SCALE).astype(BF16)
            staged[3][h][0] = (dgrad[h][1, 1] + dv).astype(BF16)
        for a in range(1, 4):
            for h in range(HEADS):
                @pl.when(ym == 0)
                def _(a=a, h=h):
                    remain(a, h, 0).start()

                @pl.when(ym > 0)
                def _(a=a, h=h):
                    leave(a, h, YS - ym, 0).start()

    for p, h in ARRIVALS:
        take_all(own[p][h].at[:, pl.ds(0, 6)], y_send.at[p, h])
    for batch in range(PER_GROUP * len(GROUPS) - AHEAD, PER_GROUP * len(GROUPS)):
        sent(batch)
    for h in range(HEADS):
        take_all(edge[h].at[0], halo_sem.at[0, h])
        take_all(edge[h].at[1], halo_sem.at[2, h])
        take_all(side[h].at[0], side_sem.at[0, h])
        take_all(side[h].at[1], side_sem.at[2, h])
        take_all(stat_got[h].at[pl.ds(0, SEQ - 1)], stat_sem.at[0, h])
    take_all(pieces, ag_sem.at[0])

    @pl.when(is_root)
    def _():
        take_all(pieces, sc_sem.at[0])

    @pl.when(me > 0)
    def _():
        take_all(t_own, t_sem.at[0])

    take_all(ml_got.at[pl.ds(0, SEQ - 1)], ml_sem.at[0])
    take_all(acc_got.at[pl.ds(0, SEQ - 1)], acc_sem.at[0])
    take_all(o0.at[pl.ds(0, SEQ - 1)], o_sem.at[0])
    take_all(rs_got.at[pl.ds(0, SEQ - 1)], rs_sem.at[0])
    for a in range(4):
        most, rest = pl.ds(0, 3 * HEADS * D), pl.ds(0, HEADS * D)
        take_all(outs[a].at[:, :, most], out_sem.at[0, a])
        take_all(outs[a].at[:, :, most], out_sem.at[1, a])
        take_all(outs[a].at[:, :, rest], out_sem.at[2, a])


def link_tables(rows, own):
    linked = rows.reshape(BLOCKS, SEQ, BLOCKS)
    block = jnp.arange(BLOCKS, dtype=jnp.int32)[:, None, None]
    peer = jnp.arange(SEQ, dtype=jnp.int32)[None, :, None]
    peer_block = jnp.arange(BLOCKS, dtype=jnp.int32)[None, None, :]
    own_id = own * BLOCKS + block
    peer_id = peer * BLOCKS + peer_block
    live = (
        (peer != own)
        & (linked > 0)
        & (own_id > 0)
        & (peer_id > 0)
        & (jnp.abs(own_id - peer_id) > 1)
    ).astype(jnp.int32)
    block_of = jnp.sum(live * block, axis=(0, 2))
    raw = jnp.where(jnp.sum(live, axis=(0, 2)) > 0, block_of, BLOCKS)
    slot = jnp.arange(SEQ, dtype=jnp.int32)
    before = (raw[None, :] < raw[:, None]) | (
        (raw[None, :] == raw[:, None]) & (slot[None, :] < slot[:, None])
    )
    rank = jnp.sum(before.astype(jnp.int32), axis=1)
    place = (rank[None, :] == slot[:, None]).astype(jnp.int32)
    order = jnp.sum(slot[None, :] * place, axis=1)
    key = jnp.sum(raw[None, :] * place, axis=1)
    same = jnp.concatenate((jnp.zeros((1,), jnp.int32), (key[1:] == key[:-1]).astype(jnp.int32)))
    bounds = jnp.arange(BLOCKS + 1, dtype=jnp.int32)
    off = jnp.sum((raw[None, :] < bounds[:, None]).astype(jnp.int32), axis=1)
    has = (off[1:] > off[:-1]).astype(jnp.int32)
    tail = off[1:]
    return block_of, order, jnp.minimum(key, BLOCKS - 1), same, tail, has, off[BLOCKS:]


def body(query_in, key_in, value_in, out_grad, pattern):
    own = lax.axis_index("seq")
    rows = lax.dynamic_slice_in_dim(pattern, own * BLOCKS, BLOCKS, 0)
    tables = link_tables(rows, own)
    shape = (2, B, YS * HEADS * D)
    arrays = [x.reshape(shape) for x in (key_in, value_in, query_in, out_grad)]
    dma = pltpu.SemaphoreType.DMA
    vm = pltpu.VMEM

    def each(shape, dtype):
        return [vm(shape, dtype) for _ in range(HEADS)]

    tile = (B, D)
    scratch = [
        each((2, BLOCKS) + tile, BF16),
        each((2, BLOCKS) + tile, BF16),
        each((2, 2) + tile, BF16),
        [vm((SEQ, 2) + tile, BF16) for _ in range(RING)],
        [each((SEQ, 2) + tile, BF16), each((SEQ, 2) + tile, BF16)],
        each((SEQ, 8, B), F32),
        each((SEQ, 8, B), F32),
        each((2, BLOCKS + 2) + tile, F32),
        each((2, 2) + tile, F32),
        [each((BLOCKS,) + tile, BF16) for _ in range(4)],
        vm((2, BLOCKS + 2) + tile, BF16),
        vm((BLOCKS, B, 4 * B), F32),
        vm((BLOCKS, B, 4 * B), BF16),
        vm((SEQ, B, B), F32),
        vm((SEQ, B, B), BF16),
        vm((SEQ + 1, B, D), F32),
        vm((SEQ + 1, B, D), F32),
        vm((BLOCKS, B, B), F32),
        vm((BLOCKS, B, B), F32),
        vm((BLOCKS, B, B), F32),
        vm((BLOCKS, B, D), F32),
        vm((BLOCKS, 8, B), F32),
        vm((4, HEADS) + tile, BF16),
        vm((4, HEADS) + tile, BF16),
        vm((HEADS, BLOCKS, B, B), BF16),
        vm((8, B), F32),
        vm((SEQ, 8, B), F32),
        vm((SEQ, 16, D), F32),
        vm((SEQ, 16, D), F32),
        vm((16, D), F32),
        vm((SEQ, 16, D), F32),
        vm((HEADS,) + tile, F32),
        vm((HEADS,) + tile, F32),
        vm((HEADS,) + tile, F32),
        vm((SEQ, 3, 16, D), F32),
        vm((SEQ, 3, 16, D), F32),
        vm((3, 16, D), F32),
        vm((SEQ, 3, 16, D), F32),
        dma((2, HEADS)),
        dma((2, HEADS)),
        dma((2, HEADS)),
        dma((3,)),
        dma((2,)),
        dma((2,)),
        dma((PER_GROUP * len(GROUPS),)),
        dma((2, HEADS)),
        dma((4, HEADS)),
        dma((4, HEADS)),
        dma((2,)),
        dma((2,)),
        dma((2,)),
        dma((2, HEADS)),
        dma((2,)),
        dma((2,)),
        dma((3, 4)),
    ]
    any_space = pl.BlockSpec(memory_space=pl.ANY)
    results = pl.pallas_call(
        kernel,
        out_shape=[jax.ShapeDtypeStruct(shape, BF16)] * 4,
        in_specs=[pl.BlockSpec(memory_space=pltpu.SMEM)] * len(tables) + [any_space] * 4,
        out_specs=[any_space] * 4,
        scratch_shapes=scratch,
        compiler_params=pltpu.CompilerParams(
            collective_id=0, has_side_effects=True, vmem_limit_bytes=62 << 20
        ),
        name="sparse_attention",
    )(*tables, *arrays)
    return tuple(x.reshape(query_in.shape) for x in results)


def solution(mesh):
    split = P(("seq", "head"), None)
    return jax.shard_map(
        body,
        mesh=mesh,
        in_specs=(split, split, split, split, P()),
        out_specs=(split, split, split, split),
        check_vma=False,
    )
```

time: 1120 us -> 298 us (0.27); the launches traced: 1100 us -> 294 us
  waiting for transfers between devices: 363 us -> 0 us
  Pallas kernels: 0 us -> 281 us
  blocking collectives: 238 us -> 0 us
  local copies, waits for them, and re-layouts: 209 us -> 8.91 us
  matrix products: 102 us -> 0 us
  starting transfers between devices: 96.9 us -> 0 us
  other arithmetic: 80.2 us -> 3.78 us
  between operations: 15.2 us -> 0.73 us
    pallas_call x0 -> x1, Pallas kernels: none -> 281 us  [body(): pl.pallas_call(kernel, out_shape=[jax.ShapeDtypeStruct(shape, BF16)] * 4,...]
    psum x2 -> x0, blocking collectives: 183 us -> none  [the longest x1 126 us: body(): global_out = lax.psum(global_acc, 'seq').astype(jnp.bfloat16)]
    psum x2 -> x0, waiting for transfers between devices: 178 us -> none  [the longest x1 89.1 us: body(): lax.psum((global_dq_part, near_dk[-block_rows:], near_dv[-block_rows:]),...]
    all_to_all x12 -> x0, waiting for transfers between devices: 165 us -> none  [the longest x1 91.1 us: body(): lax.all_to_all(part_dk, 'seq', split_axis=0, concat_axis=0, tiled=True)]
    dot_general x23 -> x0, matrix products: 102 us -> none  [the longest x1 9.83 us: body(): jnp.einsum('hnqk,nqhe->nkhe', slot_weights, slot_grad, preferred_element_...]
    all_to_all x12 -> x0, starting transfers between devices: 82.3 us -> none  [the longest x1 23.5 us: body(): lax.all_to_all(jnp.take(value_blocks, send_block, axis=0), 'seq', split_a...]
    pmax x1 -> x0, blocking collectives: 54.8 us -> none  [body(): global_top = lax.pmax(local_top, 'seq')]
    all_to_all x14 -> x0, local copies, waits for them, and re-layouts: 38 us -> none  [the longest x1 10.4 us: body(): lax.all_to_all(part_dv, 'seq', split_axis=0, concat_axis=0, tiled=True)]
  transfers between devices with their start and end apart: 18 -> 0, of which waited for: 11 -> 0; matrix products, arithmetic and copies ran while one was open for 29% -> 0% of each run, Pallas kernels for 0% -> 0%
where the time goes in v2:
time: 298 us; the launch traced here: 294 us
  Pallas kernels  281 us (94%)
  local copies, waits for them, and re-layouts  8.91 us (3%)
  other arithmetic  3.78 us (1%)
    pallas_call x1, Pallas kernels, body(): pl.pallas_call(kernel, out_shape=[jax.ShapeDtypeStruct(shape, BF16)] * 4,...  281 us
    unnamed x12, local copies, waits for them, and re-layouts  7.07 us

profile of v2, /device:TPU:32, one launch (start us, length us, event | category | flops | bytes accessed | tf_op | source)
XLA Modules:
  0.0 293.9 jit_solution(405497712531141549)
XLA Ops:
  0.7 0.1 and.43
  0.8 0.1 and.44
  0.9 0.1 add.55
  0.9 0.1 add.56
  1.0 0.1 add.58
  1.1 0.8 convert_reduce_fusion.2
  1.9 0.1 reduce_sum.72
  2.0 0.1 reduce_sum.73
  2.1 0.1 reduce_sum.69
  2.2 0.1 reduce_sum.70.block_of
  2.3 0.0 copy-start.3
  2.4 0.5 copy-done.3
  2.9 0.1 convert_reduce_fusion.1
  3.0 0.7 slice.20.live
  3.6 0.6 compare_convert_fusion.has
  4.3 0.6 slice.18.tail
  4.8 0.2 convert_reduce_fusion
  5.0 0.6 select_reduce_fusion
  5.7 0.1 slice_compare_fusion
  5.7 0.5 broadcast_minimum_fusion.key
  6.2 0.6 add_convert_fusion.same
  6.8 280.5 %sparse_attention.1 = (bf16[2,128,2048]{2,1,0:T(8,128)(2,1)}, bf16[2,128,2048]{2,1,0:T(8,128)(2,1)}, bf16[2,128,2048]{2,1,0:T(8,128)(2,1)}, bf16[2,128,2048]{2,1,0:T(8,128)(2,1)}) custom-call(s32[32]{0:T(128)} %copy-done.3, s32[32]{0:T(128)} %get-tuple-element.15.order, s32[32]{0:T(128)} %broadcast_minimum_fusion.key, s32[32]{0:T(128)} %add_convert_fusion.same, ...), custom_call_target="tpu_custom_call" | custom-call | tf_op jit(solution)/shard_map/sparse_attention/pallas_call | solution.py:754
  287.4 0.0 copy-start.2
  287.4 2.4 copy.13
  289.8 0.0 copy-done.2
  289.8 0.0 copy-start.1
  289.8 1.0 copy.14
  290.7 0.6 copy-done.1
  291.4 0.0 copy-start
  291.4 1.0 copy.15
  292.3 0.6 copy-done
  293.0 1.0 copy.16
  (7 shorter events, 0.0 us)
Async XLA Ops:
  2.3 0.5 copy-start.3
  287.4 2.4 copy-start.2
  289.8 1.6 copy-start.1
  291.4 1.6 copy-start
